TPU v7x, 256 devices: a whole 4x4x8 slice. The times are simulated.
256 devices in a mesh: row: 64 (over z, y, x_hi), col: 4 (over x_lo, core).
Axes of the slice: x: 4 (x_hi: 2, x_lo: 2; x = x_hi * 2 + x_lo), y: 4, z: 8, core: 2. Of those that a mesh axis runs over, the one named last changes fastest.
Arguments:
- measured: float32 [64, 65536], P(None, ('row', 'col')), may hold values from -4 to 4
- generated: float32 [64, 32768], P(None, ('col', 'row')), may hold values from -3 to 3
- previous: float32 [32768], P(('col', 'row')), may hold values from -2 to 14
- row_weight: float32 [65536], P(('row', 'col')), may hold values from 0.5 to 2
- col_weight: float32 [32768], P(('col', 'row')), may hold values from 0.5 to 2
Outputs:
- row_potential: float32 [65536], P(('row', 'col'))
- column_potential: float32 [32768], P(('col', 'row'))
- row_gap: float32 [65536], P(('row', 'col'))
All inputs are finite; a program needn't handle non-finite values.
Results may differ from a plain program's by a relative error of at most 0.0003.
Values sent between devices are 32-bit elements; how exact they have to be, the bound alone decides.
A program may use at most 64 MiB of HBM per device.

v0:
```python
import math

import jax
import jax.numpy as jnp
from jax import lax
from jax.sharding import PartitionSpec as P

EPSILON = 0.1


def combined_all(part, axis, combine):
    gathered = jax.tree.map(lambda a: lax.all_gather(a, axis), part)

    def take(source):
        return jax.tree.map(lambda a: lax.dynamic_index_in_dim(a, source, 0, False), gathered)

    return lax.fori_loop(
        1, lax.axis_size(axis), lambda source, state: combine(state, take(source)), take(0)
    )


def combine(first, second):
    top = jnp.maximum(first[0], second[0])
    total = first[1] * jnp.exp(first[0] - top) + second[1] * jnp.exp(second[0] - top)
    return (top, total)


def cross_costs(piece, piece_sq, right, right_sq):
    cross = lax.dot_general(
        piece,
        right,
        (((0,), (0,)), ((), ())),
        precision=lax.Precision.HIGHEST,
        preferred_element_type=jnp.float32,
    )
    return piece_sq[:, None] + right_sq[None, :] - 2.0 * cross


def body(measured, generated, previous, row_weight, col_weight):
    rows_pts, rows_mass = (
        lax.all_gather(measured, "col", axis=1, tiled=True),
        lax.all_gather(row_weight, "col", axis=0, tiled=True),
    )
    cols_pts, cols_pot, cols_mass = (
        lax.all_gather(generated, "row", axis=1, tiled=True),
        lax.all_gather(previous, "row", axis=0, tiled=True),
        lax.all_gather(col_weight, "row", axis=0, tiled=True),
    )
    width = rows_pts.shape[0]
    count = rows_pts.shape[1]
    ncols = cols_pts.shape[1]
    log_a = jnp.log(rows_mass) - math.log(count * lax.axis_size("row"))
    log_b = jnp.log(cols_mass) - math.log(ncols * lax.axis_size("col"))
    rows_sq = jnp.sum(rows_pts * rows_pts, 0)
    cols_sq = jnp.sum(cols_pts * cols_pts, 0)
    block = math.gcd(count, 256)
    nblocks = count // block
    pieces = rows_pts.reshape(width, nblocks, block).transpose(1, 0, 2)
    piece_sqs = rows_sq.reshape(nblocks, block)

    def row_lse(col_pot):

        def one(args):
            piece, piece_sq = args
            scores = (
                log_b[None, :]
                + (col_pot[None, :] - cross_costs(piece, piece_sq, cols_pts, cols_sq)) / EPSILON
            )
            top = jnp.max(scores, 1)
            return (top, jnp.sum(jnp.exp(scores - top[:, None]), 1))

        tops, totals = lax.map(one, (pieces, piece_sqs))
        tops = tops.reshape(-1)
        totals = totals.reshape(-1)
        best = lax.pmax(tops, "col")
        summed = lax.psum(totals * jnp.exp(tops - best), "col")
        return best + jnp.log(summed)

    row_pot = -EPSILON * row_lse(cols_pot)

    def column_step(carry, args):
        piece, piece_sq, piece_log, piece_pot = args
        scores = (
            piece_log[:, None]
            + (piece_pot[:, None] - cross_costs(piece, piece_sq, cols_pts, cols_sq)) / EPSILON
        )
        block_top = jnp.max(scores, 0)
        top = jnp.maximum(carry[0], block_top)
        total = carry[1] * jnp.exp(carry[0] - top) + jnp.sum(jnp.exp(scores - top[None, :]), 0)
        return ((top, total), None)

    start = (jnp.full((ncols,), -1e30, jnp.float32), jnp.zeros((ncols,), jnp.float32))
    (col_top, col_total), unused = lax.scan(
        column_step,
        start,
        (pieces, piece_sqs, log_a.reshape(nblocks, block), row_pot.reshape(nblocks, block)),
    )
    share = ncols // lax.axis_size("row")
    offset = lax.axis_index("row") * share
    best, summed = combined_all((col_top, col_total), "row", combine)
    col_pot = -EPSILON * (best + jnp.log(summed))
    col_share = lax.dynamic_slice_in_dim(col_pot, offset, share, 0)
    gap = row_pot / EPSILON + row_lse(col_pot)
    row_share = count // lax.axis_size("col")
    row_offset = lax.axis_index("col") * row_share
    return (
        lax.dynamic_slice_in_dim(row_pot, row_offset, row_share, 0),
        col_share,
        lax.dynamic_slice_in_dim(gap, row_offset, row_share, 0),
    )


def solution(mesh):
    placed = (
        P(None, ("row", "col")),
        P(None, ("col", "row")),
        P(("col", "row")),
        P(("row", "col")),
        P(("col", "row")),
    )
    return jax.shard_map(
        body,
        mesh=mesh,
        in_specs=placed,
        out_specs=(P(("row", "col")), P(("col", "row")), P(("row", "col"))),
        check_vma=False,
    )
```

profile of v0, /device:TPU:1, one launch (start us, length us, event | category | flops | bytes accessed | tf_op | source)
XLA Modules:
  0.0 914.4 jit_solution(14259656842406431104)
XLA Ops:
  8.0 9.1 all_gather.29
  17.3 5.3 all-gather.4
  22.6 154.2 %all-gather.2 = f32[64,1,128]{2,1,0:T(1,128)S(1)} all-gather(f32[1,1,128]{2,1,0:T(1,128)} %bitcast.106), channel_id=1, replica_groups=mesh['row'=64,'col'=4] {'row'}, dimensions={0}, use_global_device_ids=true | all-gather | bytes 33280 | tf_op jit(solution)/shard_map/all_gather | solution.py:47
  176.8 145.5 %all-gather.3 = f32[64,1,128]{2,1,0:T(1,128)S(1)} all-gather(f32[1,1,128]{2,1,0:T(1,128)} %bitcast.107), channel_id=1, replica_groups=mesh['row'=64,'col'=4] {'row'}, dimensions={0}, use_global_device_ids=true | all-gather | bytes 33280 | tf_op jit(solution)/shard_map/all_gather | solution.py:46
  324.2 66.4 %while.54 = (s32[]{:T(128)}, f32[4,256]{1,0:T(4,128)S(1)}, f32[4,256]{1,0:T(4,128)S(1)}, f32[8192]{0:T(1024)S(1)}, f32[8192]{0:T(1024)S(1)}, /*index=5*/f32[4,25...) while((s32[]{:T(128)}, f32[4,256]{1,0:T(4,128)S(1)}, ...), condition=%wide.region_5.6_spmd, body=%wide.region_2.5_spmd.sunk | while | flops 1629486592 | bytes 19048580 | solution.py:72
  324.2 11.9 %fusion.36 = (f32[256]{0:T(256)S(1)}, f32[256,8192]{1,0:T(8,128)}) fusion(f32[64,8192]{1,0:T(8,128)} %get-tuple-element.698, f32[4,64,256]{2,1,0:T(8,128)S(1)} %get-tuple-element.697, s32[]{:T(128)S(6)} %copy.28, f32[8192]{0:T(1024)S(1)} %get-tuple-element.696, f32[256]{0:T(256)S(1)} %bitcast.94, f32[8192]{0:T(1024)S(1)} %get-tuple-element.694, ...), kind=kOutput, calls=%fused_computation.49.clone.1 | convolution fusion | flops 1625292544 | bytes 10651652 | tf_op jit(solution)/shard_map/while/body/eval_jaxpr/dot_general | solution.py:29
  336.1 4.6 exponential_reduce_fusion.6
  340.8 11.9 %fusion.36 = (f32[256]{0:T(256)S(1)}, f32[256,8192]{1,0:T(8,128)}) fusion(f32[64,8192]{1,0:T(8,128)} %get-tuple-element.698, f32[4,64,256]{2,1,0:T(8,128)S(1)} %get-tuple-element.697, s32[]{:T(128)S(6)} %copy.28, f32[8192]{0:T(1024)S(1)} %get-tuple-element.696, f32[256]{0:T(256)S(1)} %bitcast.94, f32[8192]{0:T(1024)S(1)} %get-tuple-element.694, ...), kind=kOutput, calls=%fused_computation.49.clone.1 | convolution fusion | flops 1625292544 | bytes 10651652 | tf_op jit(solution)/shard_map/while/body/eval_jaxpr/dot_general | solution.py:29
  357.4 11.9 %fusion.36 = (f32[256]{0:T(256)S(1)}, f32[256,8192]{1,0:T(8,128)}) fusion(f32[64,8192]{1,0:T(8,128)} %get-tuple-element.698, f32[4,64,256]{2,1,0:T(8,128)S(1)} %get-tuple-element.697, s32[]{:T(128)S(6)} %copy.28, f32[8192]{0:T(1024)S(1)} %get-tuple-element.696, f32[256]{0:T(256)S(1)} %bitcast.94, f32[8192]{0:T(1024)S(1)} %get-tuple-element.694, ...), kind=kOutput, calls=%fused_computation.49.clone.1 | convolution fusion | flops 1625292544 | bytes 10651652 | tf_op jit(solution)/shard_map/while/body/eval_jaxpr/dot_general | solution.py:29
  369.3 4.6 exponential_reduce_fusion.6
  374.0 11.9 %fusion.36 = (f32[256]{0:T(256)S(1)}, f32[256,8192]{1,0:T(8,128)}) fusion(f32[64,8192]{1,0:T(8,128)} %get-tuple-element.698, f32[4,64,256]{2,1,0:T(8,128)S(1)} %get-tuple-element.697, s32[]{:T(128)S(6)} %copy.28, f32[8192]{0:T(1024)S(1)} %get-tuple-element.696, f32[256]{0:T(256)S(1)} %bitcast.94, f32[8192]{0:T(1024)S(1)} %get-tuple-element.694, ...), kind=kOutput, calls=%fused_computation.49.clone.1 | convolution fusion | flops 1625292544 | bytes 10651652 | tf_op jit(solution)/shard_map/while/body/eval_jaxpr/dot_general | solution.py:29
  385.9 4.6 exponential_reduce_fusion.6
  390.6 61.1 %pmax.14 = f32[1024]{0:T(1024)S(1)} all-reduce(f32[1024]{0:T(1024)S(1)} %bitcast.87), channel_id=1, replica_groups=mesh['row'=64,'col'=4] {'col'}, use_global_device_ids=true, to_apply=%region_6.7 | all-reduce | flops 1024 | bytes 8192 | tf_op jit(solution)/shard_map/pmax | solution.py:75
  451.8 6.0 psum.14
  457.8 66.1 %while.57 = (s32[]{:T(128)}, f32[8192]{0:T(1024)S(1)}, f32[8192]{0:T(1024)S(1)}, f32[4,256]{1,0:T(4,128)S(1)}, f32[4,256]{1,0:T(4,128)S(1)}, /*index=5*/f32[4,25...) while((s32[]{:T(128)}, f32[8192]{0:T(1024)S(1)}, ...), condition=%wide.region_11.12_spmd.clone, body=%wide.region_8.11_spmd.clone.sunk | while | flops 1629528064 | bytes 19408012 | solution.py:93
  457.8 11.8 %fusion.40 = (f32[8192]{0:T(1024)S(1)}, f32[256,8192]{1,0:T(8,128)}) fusion(f32[64,8192]{1,0:T(8,128)} %get-tuple-element.731, f32[4,64,256]{2,1,0:T(8,128)S(1)} %get-tuple-element.730, s32[]{:T(128)S(6)} %copy.37, f32[8192]{0:T(1024)S(1)} %get-tuple-element.729, f32[256]{0:T(256)S(1)} %bitcast.96, f32[256]{0:T(256)S(1)} %bitcast.97, ...), kind=kOutput, calls=%fused_computation.51.clone.1 | convolution fusion | flops 1625284608 | bytes 10619908 | tf_op jit(solution)/shard_map/while/body/eval_jaxpr/dot_general | solution.py:29
  474.3 11.8 %fusion.40 = (f32[8192]{0:T(1024)S(1)}, f32[256,8192]{1,0:T(8,128)}) fusion(f32[64,8192]{1,0:T(8,128)} %get-tuple-element.731, f32[4,64,256]{2,1,0:T(8,128)S(1)} %get-tuple-element.730, s32[]{:T(128)S(6)} %copy.37, f32[8192]{0:T(1024)S(1)} %get-tuple-element.729, f32[256]{0:T(256)S(1)} %bitcast.96, f32[256]{0:T(256)S(1)} %bitcast.97, ...), kind=kOutput, calls=%fused_computation.51.clone.1 | convolution fusion | flops 1625284608 | bytes 10619908 | tf_op jit(solution)/shard_map/while/body/eval_jaxpr/dot_general | solution.py:29
  490.8 11.8 %fusion.40 = (f32[8192]{0:T(1024)S(1)}, f32[256,8192]{1,0:T(8,128)}) fusion(f32[64,8192]{1,0:T(8,128)} %get-tuple-element.731, f32[4,64,256]{2,1,0:T(8,128)S(1)} %get-tuple-element.730, s32[]{:T(128)S(6)} %copy.37, f32[8192]{0:T(1024)S(1)} %get-tuple-element.729, f32[256]{0:T(256)S(1)} %bitcast.96, f32[256]{0:T(256)S(1)} %bitcast.97, ...), kind=kOutput, calls=%fused_computation.51.clone.1 | convolution fusion | flops 1625284608 | bytes 10619908 | tf_op jit(solution)/shard_map/while/body/eval_jaxpr/dot_general | solution.py:29
  507.4 11.8 %fusion.40 = (f32[8192]{0:T(1024)S(1)}, f32[256,8192]{1,0:T(8,128)}) fusion(f32[64,8192]{1,0:T(8,128)} %get-tuple-element.731, f32[4,64,256]{2,1,0:T(8,128)S(1)} %get-tuple-element.730, s32[]{:T(128)S(6)} %copy.37, f32[8192]{0:T(1024)S(1)} %get-tuple-element.729, f32[256]{0:T(256)S(1)} %bitcast.96, f32[256]{0:T(256)S(1)} %bitcast.97, ...), kind=kOutput, calls=%fused_computation.51.clone.1 | convolution fusion | flops 1625284608 | bytes 10619908 | tf_op jit(solution)/shard_map/while/body/eval_jaxpr/dot_general | solution.py:29
  525.9 109.6 %all-gather.11.cloned.1.call-done = f32[524288]{0:T(1024)} async-done(((f32[8192]{0:T(1024)}), f32[524288]{0:T(1024)}) %all-gather.11.cloned.1.call-update) | async-done | bytes 2097168 | tf_op jit(solution)/shard_map/all_gather | solution.py:12
  637.3 117.2 %all-gather.13.cloned.1.call-done = f32[524288]{0:T(1024)} async-done(((f32[8192]{0:T(1024)}), f32[524288]{0:T(1024)}) %all-gather.13.cloned.1.call-update) | async-done | bytes 2097168 | tf_op jit(solution)/shard_map/all_gather | solution.py:12
  758.0 67.1 %while.55 = (s32[]{:T(128)}, f32[8192]{0:T(1024)S(1)}, f32[8192]{0:T(1024)S(1)}, f32[64,8192]{1,0:T(8,128)S(1)}, f32[64,8192]{1,0:T(8,128)}, /*index=5*/s32[]{:T(128)}, s32[]{:T(128)}, s32[]{:T(128)}) while((s32[]{:T(128)}, f32[8192]{0:T(1024)S(1)}, f32[8192]{0:T(1024)S(1)}, f32[64,8192]{1,0:T(8,128)S(1)}, f32[64,8192]{1,0:T(8,128)}, ...), condition=%wide.region_13.14_spmd, body=%wide.region_12.13_spmd.sunk | while | flops 49157 | bytes 327811 | solution.py:17
  825.7 66.5 %while.56 = (s32[]{:T(128)}, f32[4,256]{1,0:T(4,128)S(1)}, f32[4,256]{1,0:T(4,128)S(1)}, f32[8192]{0:T(1024)S(1)}, f32[8192]{0:T(1024)S(1)}, /*index=5*/f32[4,25...) while((s32[]{:T(128)}, f32[4,256]{1,0:T(4,128)S(1)}, ...), condition=%wide.region_17.18_spmd, body=%wide.region_14.17_spmd.sunk | while | flops 1629486592 | bytes 19048580 | solution.py:72
  825.7 11.9 %fusion.38 = (f32[256]{0:T(256)S(1)}, f32[256,8192]{1,0:T(8,128)}) fusion(f32[64,8192]{1,0:T(8,128)} %get-tuple-element.788, f32[4,64,256]{2,1,0:T(8,128)S(1)} %get-tuple-element.787, s32[]{:T(128)S(6)} %copy.55, f32[8192]{0:T(1024)S(1)} %get-tuple-element.786, f32[256]{0:T(256)S(1)} %bitcast.95, f32[8192]{0:T(1024)S(1)} %get-tuple-element.784, ...), kind=kOutput, calls=%fused_computation.50.clone.1 | convolution fusion | flops 1625292544 | bytes 10651652 | tf_op jit(solution)/shard_map/while/body/eval_jaxpr/dot_general | solution.py:29
  837.6 4.6 exponential_reduce_fusion.7
  842.3 11.9 %fusion.38 = (f32[256]{0:T(256)S(1)}, f32[256,8192]{1,0:T(8,128)}) fusion(f32[64,8192]{1,0:T(8,128)} %get-tuple-element.788, f32[4,64,256]{2,1,0:T(8,128)S(1)} %get-tuple-element.787, s32[]{:T(128)S(6)} %copy.55, f32[8192]{0:T(1024)S(1)} %get-tuple-element.786, f32[256]{0:T(256)S(1)} %bitcast.95, f32[8192]{0:T(1024)S(1)} %get-tuple-element.784, ...), kind=kOutput, calls=%fused_computation.50.clone.1 | convolution fusion | flops 1625292544 | bytes 10651652 | tf_op jit(solution)/shard_map/while/body/eval_jaxpr/dot_general | solution.py:29
  854.3 4.6 exponential_reduce_fusion.7
  859.0 11.9 %fusion.38 = (f32[256]{0:T(256)S(1)}, f32[256,8192]{1,0:T(8,128)}) fusion(f32[64,8192]{1,0:T(8,128)} %get-tuple-element.788, f32[4,64,256]{2,1,0:T(8,128)S(1)} %get-tuple-element.787, s32[]{:T(128)S(6)} %copy.55, f32[8192]{0:T(1024)S(1)} %get-tuple-element.786, f32[256]{0:T(256)S(1)} %bitcast.95, f32[8192]{0:T(1024)S(1)} %get-tuple-element.784, ...), kind=kOutput, calls=%fused_computation.50.clone.1 | convolution fusion | flops 1625292544 | bytes 10651652 | tf_op jit(solution)/shard_map/while/body/eval_jaxpr/dot_general | solution.py:29
  870.9 4.6 exponential_reduce_fusion.7
  875.6 11.9 %fusion.38 = (f32[256]{0:T(256)S(1)}, f32[256,8192]{1,0:T(8,128)}) fusion(f32[64,8192]{1,0:T(8,128)} %get-tuple-element.788, f32[4,64,256]{2,1,0:T(8,128)S(1)} %get-tuple-element.787, s32[]{:T(128)S(6)} %copy.55, f32[8192]{0:T(1024)S(1)} %get-tuple-element.786, f32[256]{0:T(256)S(1)} %bitcast.95, f32[8192]{0:T(1024)S(1)} %get-tuple-element.784, ...), kind=kOutput, calls=%fused_computation.50.clone.1 | convolution fusion | flops 1625292544 | bytes 10651652 | tf_op jit(solution)/shard_map/while/body/eval_jaxpr/dot_general | solution.py:29
  892.2 9.0 pmax.15
  901.3 6.0 psum.15
  (219 shorter events, 105.4 us)
Async XLA Ops:
  7.2 315.2 %all-gather.9.cloned.1.call-start = ((), (), s32[]{:S(2)}) async-start(), calls=%async_computation | async-start | bytes 2129920 | tf_op jit(solution)/shard_map/all_gather | solution.py:45
  7.9 627.6 %all-gather.11.cloned.1.call-start = ((), (), s32[]{:S(2)}) async-start(), calls=%async_computation.1 | async-start | bytes 2129920 | tf_op jit(solution)/shard_map/all_gather | solution.py:12
  523.9 0.6 copy-start
  523.9 0.7 copy-start.1
  524.5 230.0 %all-gather.13.cloned.1.call-start = ((), (), s32[]{:S(2)}) async-start(), calls=%async_computation.2 | async-start | bytes 2129920 | tf_op jit(solution)/shard_map/all_gather | solution.py:12
  635.5 122.5 %slice-start = ((f32[524288]{0:T(1024)}), f32[8192]{0:T(1024)S(1)}, s32[]{:S(2)}) async-start(f32[524288]{0:T(1024)} %all-gather.11.cloned.1.call-done), calls=%async_computation.3 | async-start | bytes 65536 | tf_op jit(solution)/shard_map/jit(dynamic_index_in_dim)/dynamic_slice | solution.py:15
Sparse Core Ops, SparseCore 0:
  11.4 111.3 all-gather.8
  524.6 110.8 all-gather.10
  639.1 115.3 all-gather.12
where the time goes:
time: 917 us; the launch traced here: 914 us
  blocking collectives  396 us (43%)
  waiting for transfers between devices  228 us (25%)
  matrix products  142 us (15%)
  local copies, waits for them, and re-layouts  71.8 us (8%)
  other arithmetic  60 us (7%)
  between operations  13.9 us (2%)
    all_gather x2, waiting for transfers between devices, combined_all(): gathered = jax.tree.map(lambda a: lax.all_gather(a, axis), part)  227 us
    all_gather x1, blocking collectives, body(): lax.all_gather(col_weight, 'row', axis=0, tiled=True)  154 us
    all_gather x1, blocking collectives, body(): lax.all_gather(previous, 'row', axis=0, tiled=True)  146 us
    dot_general x12, matrix products, cross_costs(): lax.dot_general(piece, right, (((0,), (0,)), ((), ())), precision=lax.Pre...  142 us
    pmax x2, blocking collectives, row_lse(): best = lax.pmax(tops, 'col')  70.2 us
    dynamic_slice x66, local copies, waits for them, and re-layouts, take(): lax.dynamic_index_in_dim(a, source, 0, False)  63.9 us
    reduce_sum x8, other arithmetic, one(): return (top, jnp.sum(jnp.exp(scores - top[:, None]), 1))  37.1 us
    reduce_sum x4, other arithmetic, column_step(): jnp.sum(jnp.exp(scores - top[None, :]), 0)  18.4 us
  transfers between devices with their start and end apart: 3, of which 2 were waited for; matrix products, arithmetic and copies ran while one was open for 0% of the time, Pallas kernels for 0%

commit v1 on v0

v1 whole, which is shorter than its diff:
```python
import functools
import math

import jax
import jax.numpy as jnp
from jax import lax
from jax.experimental import pallas as pl
from jax.experimental.pallas import tpu as pltpu
from jax.sharding import PartitionSpec as P

EPSILON = 0.1
LOG2E = 1.0 / math.log(2.0)
LN2 = math.log(2.0)
MESH = pl.DeviceIdType.MESH
F32 = jnp.float32
BF16 = jnp.bfloat16

GRID = {"z": 8, "y": 4, "xh": 2, "xl": 2}
XB = 256
YB = 128
DIM = 64


def kernel(
    measured,
    generated,
    previous,
    row_weight,
    col_weight,
    row_out,
    col_out,
    gap_out,
    xraw,
    yraw,
    yt,
    xaug,
    scores,
    cstat,
    sstat,
    row_stat_out,
    row_stat_in,
    rbuf,
    col_stat_out,
    col_stat_in,
    qbuf,
    w_out,
    w_in,
    x_send,
    x_recv,
    y_send,
    y_recv,
    row_send,
    row_recv,
    r_send,
    r_recv,
    col_send,
    col_recv,
    q_send,
    q_recv,
    w_send,
    w_recv,
):
    NZ, NY, NXH, NXL = GRID["z"], GRID["y"], GRID["xh"], GRID["xl"]
    NX = NXH * NXL
    NQ, NP = NX * NY, NZ * 2
    NJ = NP * YB
    NI = NQ * XB
    NL = NI // 128
    ndev = NQ * NP

    row = lax.axis_index("row")
    col = lax.axis_index("col")
    z = row // (NY * NXH)
    y = (row // NXH) % NY
    x = (row % NXH) * NXL + col // 2
    core = col % 2

    def device(dz, dy, dx, dc):
        zz, yy, xx = (z + dz) % NZ, (y + dy) % NY, (x + dx) % NX
        return ((zz * NY + yy) * NXH + xx // NXL, (xx % NXL) * 2 + (core + dc) % 2)

    def xslot(dy, dx):
        return (dy % NY) * NX + dx % NX

    def yslot(dz, dc):
        return (dz % NZ) * 2 + dc % 2

    def copy(src, dst, send, recv, dev):
        return pltpu.make_async_remote_copy(
            src_ref=src, dst_ref=dst, send_sem=send, recv_sem=recv, device_id=dev, device_id_type=MESH
        )

    plane = [(dy, dx) for dy in range(NY) for dx in range(NX) if (dy, dx) != (0, 0)]
    line = [(dz, dc) for dz in range(NZ) for dc in range(2) if (dz, dc) != (0, 0)]

    barrier = pltpu.get_barrier_semaphore()
    for dy, dx in plane:
        pl.semaphore_signal(barrier, inc=1, device_id=device(0, dy, dx, 0), device_id_type=MESH)
    for dz, dc in line:
        pl.semaphore_signal(barrier, inc=1, device_id=device(dz, 0, 0, dc), device_id_type=MESH)

    scale = 2.0 * LOG2E / EPSILON
    xraw[0] = measured[...] * scale
    gen = generated[...]
    log_b = jnp.log(col_weight[...]) - math.log(YB * ndev)
    ysq = jnp.sum(gen * gen, axis=0, keepdims=True)
    u = (log_b + (previous[...] - ysq) / EPSILON) * LOG2E
    yraw[0, 0:DIM] = gen
    yraw[0, DIM : DIM + 8] = jnp.broadcast_to(u, (8, YB))
    log_a = jnp.log(row_weight[...]) - math.log(XB * ndev)
    xsq = jnp.sum(measured[...] * measured[...], axis=0, keepdims=True)

    pl.semaphore_wait(barrier, len(plane) + len(line))

    pending = []

    def start(c):
        c.start()
        pending.append(c)

    half = DIM // 2
    counter = [0]

    def send_x(slot, part, dst_slot, dev):
        at = pl.ds(part * half, half)
        n = counter[0]
        counter[0] += 1
        start(copy(xraw.at[slot, at], xraw.at[dst_slot, at], x_send.at[n], x_recv.at[dst_slot, part], dev))

    def wait_x(slot, part):
        at = pl.ds(part * half, half)
        copy(xraw.at[slot, at], xraw.at[slot, at], x_send.at[0], x_recv.at[slot, part], device(0, 0, 1, 0)).wait_recv()

    def send_y(n, slot, dst_slot, dev):
        start(copy(yraw.at[slot], yraw.at[dst_slot], y_send.at[n], y_recv.at[dst_slot], dev))

    def wait_y(slot):
        copy(yraw.at[slot], yraw.at[slot], y_send.at[0], y_recv.at[slot], device(0, 0, 0, 1)).wait_recv()

    def near_first(n):
        return sorted(range(1, n), key=lambda d: min(d, n - d))

    for ez in near_first(NZ):
        send_y(ez, 0, yslot(-ez, 0), device(ez, 0, 0, 0))
    send_y(0, 0, yslot(0, 1), device(0, 0, 0, 1))
    for e in near_first(max(NX, NY)):
        if e < NX:
            send_x(0, 0, xslot(0, -e), device(0, 0, e, 0))
        if e < NY:
            send_x(0, 1, xslot(-e, 0), device(0, e, 0, 0))
    for e in near_first(max(NX, NY)):
        if e < NX:
            send_x(0, 1, xslot(0, -e), device(0, 0, e, 0))
        if e < NY:
            send_x(0, 0, xslot(-e, 0), device(0, e, 0, 0))

    def forward_x(d):
        if d < NX:
            wait_x(xslot(0, d), 0)
            for ey in near_first(NY):
                send_x(xslot(0, d), 0, xslot(-ey, d), device(0, ey, 0, 0))
        if d < NY:
            wait_x(xslot(d, 0), 1)
            for ex in near_first(NX):
                send_x(xslot(d, 0), 1, xslot(d, -ex), device(0, 0, ex, 0))

    def forward_y(dz):
        wait_y(yslot(dz, 0))
        send_y(NZ + dz, yslot(dz, 0), yslot(dz, 1), device(0, 0, 0, 1))

    xs, ys = near_first(max(NX, NY)), near_first(NZ)
    for k in range(max(len(xs), len(ys))):
        if k < len(xs):
            forward_x(xs[k])
        if k < len(ys):
            forward_y(ys[k])

    xaug[3 * DIM :] = jnp.ones((DIM, XB), BF16)

    def split(v):
        hi = v.astype(BF16).astype(F32)
        return hi, v - hi

    def turn_y(slot):
        v = yraw[slot, 0:DIM]
        hi, lo = split(v)
        t = yraw[slot, DIM : DIM + 8]
        t1, rest = split(t)
        t2, t3 = split(rest)
        sub = lax.broadcasted_iota(jnp.int32, (8, YB), 0)
        extra = jnp.where(sub == 0, t1, jnp.where(sub == 1, t2, jnp.where(sub == 2, t3, 0.0)))
        at = pl.ds(pl.multiple_of(slot * YB, YB), YB)
        yt[at, 0 : 2 * DIM] = jnp.concatenate([hi, hi], axis=0).T.astype(BF16)
        yt[at, 2 * DIM :] = jnp.concatenate([lo, extra, jnp.zeros((DIM - 8, YB), F32)], axis=0).T.astype(BF16)

    for dz in range(NZ):
        wait_y(yslot(dz, 1))
    for dy, dx in plane:
        for part in range(2):
            if not ((dy == 0 and part == 0) or (dx == 0 and part == 1)):
                wait_x(xslot(dy, dx), part)

    def turn_loop(slot, carry):
        turn_y(slot)
        return carry

    lax.fori_loop(0, NP, turn_loop, 0)

    CH = 256
    sub256 = lax.broadcasted_iota(jnp.int32, (8, XB), 0)
    sub128 = lax.broadcasted_iota(jnp.int32, (8, YB), 0)

    def row_block(b):
        v = xraw[b]
        hi = v.astype(BF16)
        lo = (v - hi.astype(F32)).astype(BF16)
        xaug[0:DIM] = hi
        xaug[DIM : 2 * DIM] = lo
        xaug[2 * DIM : 3 * DIM] = hi
        lanes = pl.ds(pl.multiple_of(b * XB, XB), XB)
        top = jnp.full((8, XB), -3e38, F32)
        total = jnp.zeros((8, XB), F32)
        for c in range(NJ // CH):
            res = jnp.dot(yt[c * CH : (c + 1) * CH], xaug[...], preferred_element_type=F32)
            scores[c * CH : (c + 1) * CH, lanes] = res
            r3 = res.reshape(CH // 8, 8, XB)
            new = jnp.maximum(top, jnp.max(r3, axis=0))
            total = total * jnp.exp2(top - new) + jnp.sum(jnp.exp2(r3 - new[None]), axis=0)
            top = new
        best = jnp.max(top, axis=0, keepdims=True)
        summed = jnp.sum(total * jnp.exp2(top - best), axis=0, keepdims=True)
        return jnp.where(sub256 < 4, best, summed)

    def row_loop(b, carry):
        row_stat_out[b] = row_block(b)
        dy, dx = b // NX, b % NX
        dst = ((NY - dy) % NY) * NX + (NX - dx) % NX
        copy(row_stat_out.at[b], row_stat_in.at[dst], row_send.at[b], row_recv.at[dst], device(0, dy, dx, 0)).start()
        return carry

    lax.fori_loop(1, NQ, row_loop, 0)
    row_stat_in[0] = row_block(0)

    def wait_in(buf, slot, send, recv):
        copy(buf.at[slot], buf.at[slot], send.at[slot], recv.at[slot], device(0, 0, 1, 0)).wait_recv()

    def wait_out(buf, slot, send, recv):
        copy(buf.at[slot], buf.at[slot], send.at[slot], recv.at[slot], device(0, 0, 1, 0)).wait_send()

    for k in range(1, NQ):
        wait_in(row_stat_in, k, row_send, row_recv)

    def combined(ref, n):
        stats = [ref[k] for k in range(n)]
        best = functools.reduce(jnp.maximum, [s[0:1] for s in stats])
        summed = functools.reduce(jnp.add, [s[4:5] * jnp.exp2(s[0:1] - best) for s in stats])
        return best + jnp.log(summed) * LOG2E

    row_lse = combined(row_stat_in, NQ)
    rbuf[0] = jnp.broadcast_to(log_a * LOG2E - row_lse, (8, XB))
    for dy, dx in plane:
        s, d = xslot(dy, dx), xslot(-dy, -dx)
        copy(rbuf.at[0], rbuf.at[d], r_send.at[s], r_recv.at[d], device(0, dy, dx, 0)).start()
    row_out[...] = xsq - (EPSILON * LN2) * row_lse
    for k in range(1, NQ):
        wait_in(rbuf, k, r_send, r_recv)

    eye = lax.broadcasted_iota(jnp.int32, (YB, YB), 0) == lax.broadcasted_iota(jnp.int32, (YB, YB), 1)

    def across(v):
        return jnp.sum(jnp.where(eye, v, 0.0), axis=0, keepdims=True)

    def col_block(b):
        base = pl.multiple_of(b * YB, YB)

        def tile(t, carry):
            at = pl.ds(pl.multiple_of(base + t * 8, 8), 8)
            vals = [
                scores[at, l * 128 : (l + 1) * 128] + rbuf[l // 2, :, (l % 2) * 128 : (l % 2 + 1) * 128]
                for l in range(NL)
            ]
            tops = vals
            while len(tops) > 1:
                tops = [jnp.maximum(tops[i], tops[i + 1]) for i in range(0, len(tops), 2)]
            top = tops[0]
            parts = []
            for l in range(NL):
                p = jnp.exp2(vals[l] - top)
                scores[at, l * 128 : (l + 1) * 128] = p
                if l < 4:
                    parts.append(p)
                else:
                    parts[l % 4] = parts[l % 4] + p
            cstat[at, :] = top
            sstat[pl.ds(pl.multiple_of(t * 8, 8), 8), :] = functools.reduce(jnp.add, parts)
            return carry

        lax.fori_loop(0, YB // 8, tile, 0, unroll=4)
        c = cstat[pl.ds(base, YB), :]
        best = jnp.max(c, axis=1, keepdims=True)
        summed = jnp.sum(sstat[...] * jnp.exp2(c - best), axis=1, keepdims=True)
        return jnp.where(sub128 < 4, across(best), across(summed))

    def col_loop(b, carry):
        col_stat_out[b] = col_block(b)
        dz, dc = b // 2, b % 2
        dst = ((NZ - dz) % NZ) * 2 + dc
        copy(col_stat_out.at[b], col_stat_in.at[dst], col_send.at[b], col_recv.at[dst], device(dz, 0, 0, dc)).start()
        return carry

    lax.fori_loop(1, NP, col_loop, 0)
    col_stat_in[0] = col_block(0)
    for k in range(1, NP):
        wait_in(col_stat_in, k, col_send, col_recv)
    col_lse = combined(col_stat_in, NP)
    qbuf[0] = jnp.broadcast_to(log_b * LOG2E - col_lse, (8, YB))
    for dz, dc in line:
        s, d = yslot(dz, dc), yslot(-dz, dc)
        copy(qbuf.at[0], qbuf.at[d], q_send.at[s], q_recv.at[d], device(dz, 0, 0, dc)).start()
    col_out[...] = previous[...] + EPSILON * log_b - (EPSILON * LN2) * col_lse

    def gap_block(b, acc):
        base = pl.multiple_of(b * YB, YB)
        q = jnp.sum(jnp.where(eye, qbuf[b, 0:1], 0.0), axis=1, keepdims=True)
        sstat[...] = jnp.exp2(cstat[pl.ds(base, YB), :] + q)

        def tile(t, acc):
            at = pl.ds(pl.multiple_of(base + t * 8, 8), 8)
            g = sstat[pl.ds(pl.multiple_of(t * 8, 8), 8), :]
            return [acc[l] + scores[at, l * 128 : (l + 1) * 128] * g for l in range(NL)]

        return lax.fori_loop(0, YB // 8, tile, acc, unroll=4)

    def gap_loop(b, acc):
        wait_in(qbuf, b, q_send, q_recv)
        return gap_block(b, acc)

    acc = gap_block(0, [jnp.zeros((8, 128), F32) for _ in range(NL)])
    acc = lax.fori_loop(1, NP, gap_loop, acc)
    for k in range(NQ):
        for h in range(2):
            total = jnp.sum(acc[2 * k + h], axis=0, keepdims=True)
            at = slice(h * 128, (h + 1) * 128)
            if k == 0:
                w_in[0, :, at] = jnp.broadcast_to(total, (8, 128))
            else:
                w_out[k, :, at] = jnp.broadcast_to(total, (8, 128))
        if k > 0:
            dy, dx = k // NX, k % NX
            d = xslot(-dy, -dx)
            copy(w_out.at[k], w_in.at[d], w_send.at[k], w_recv.at[d], device(0, dy, dx, 0)).start()

    for c in pending:
        c.wait_send()
    for k in range(1, NQ):
        wait_out(row_stat_out, k, row_send, row_recv)
        wait_out(rbuf, k, r_send, r_recv)
    for k in range(1, NP):
        wait_out(col_stat_out, k, col_send, col_recv)
        wait_out(qbuf, k, q_send, q_recv)

    for k in range(1, NQ):
        wait_in(w_in, k, w_send, w_recv)
    mass = functools.reduce(jnp.add, [w_in[k, 0:1] for k in range(NQ)])
    gap_out[...] = jnp.log(mass) - log_a
    for k in range(1, NQ):
        wait_out(w_out, k, w_send, w_recv)


def body(measured, generated, previous, row_weight, col_weight):
    NQ = GRID["y"] * GRID["xh"] * GRID["xl"]
    NP = GRID["z"] * 2
    NJ, NI = NP * YB, NQ * XB
    dma = pltpu.SemaphoreType.DMA
    row, col, gap = pl.pallas_call(
        kernel,
        out_shape=(
            jax.ShapeDtypeStruct((1, XB), F32),
            jax.ShapeDtypeStruct((1, YB), F32),
            jax.ShapeDtypeStruct((1, XB), F32),
        ),
        in_specs=[pl.BlockSpec(memory_space=pltpu.VMEM)] * 5,
        out_specs=(pl.BlockSpec(memory_space=pltpu.VMEM),) * 3,
        scratch_shapes=[
            pltpu.VMEM((NQ, DIM, XB), F32),
            pltpu.VMEM((NP, DIM + 8, YB), F32),
            pltpu.VMEM((NJ, 4 * DIM), BF16),
            pltpu.VMEM((4 * DIM, XB), BF16),
            pltpu.VMEM((NJ, NI), F32),
            pltpu.VMEM((NJ, 128), F32),
            pltpu.VMEM((YB, 128), F32),
            pltpu.VMEM((NQ, 8, XB), F32),
            pltpu.VMEM((NQ, 8, XB), F32),
            pltpu.VMEM((NQ, 8, XB), F32),
            pltpu.VMEM((NP, 8, YB), F32),
            pltpu.VMEM((NP, 8, YB), F32),
            pltpu.VMEM((NP, 8, YB), F32),
            pltpu.VMEM((NQ, 8, XB), F32),
            pltpu.VMEM((NQ, 8, XB), F32),
            dma((2 * NQ,)),
            dma((NQ, 2)),
            dma((NP,)),
            dma((NP,)),
            dma((NQ,)),
            dma((NQ,)),
            dma((NQ,)),
            dma((NQ,)),
            dma((NP,)),
            dma((NP,)),
            dma((NP,)),
            dma((NP,)),
            dma((NQ,)),
            dma((NQ,)),
        ],
        compiler_params=pltpu.CompilerParams(
            collective_id=0, has_side_effects=True, vmem_limit_bytes=48 * 1024 * 1024
        ),
    )(
        measured,
        generated,
        previous.reshape(1, YB),
        row_weight.reshape(1, XB),
        col_weight.reshape(1, YB),
    )
    return row.reshape(XB), col.reshape(YB), gap.reshape(XB)


def solution(mesh):
    placed = (
        P(None, ("row", "col")),
        P(None, ("col", "row")),
        P(("col", "row")),
        P(("row", "col")),
        P(("col", "row")),
    )
    return jax.shard_map(
        body,
        mesh=mesh,
        in_specs=placed,
        out_specs=(P(("row", "col")), P(("col", "row")), P(("row", "col"))),
        check_vma=False,
    )
```

time: 917 us -> 74.5 us (0.08)
  blocking collectives: 396 us -> 0 us
  waiting for transfers between devices: 228 us -> 0 us
  matrix products: 142 us -> 0 us
  Pallas kernels: 0 us -> 69.7 us
  local copies, waits for them, and re-layouts: 71.8 us -> 3.91 us
  other arithmetic: 60 us -> 0 us
  between operations: 13.9 us -> 0.67 us
    all_gather x4 -> x0, blocking collectives: 314 us -> none  [the longest x1 154 us: body(): lax.all_gather(col_weight, 'row', axis=0, tiled=True)]
    all_gather x3 -> x0, waiting for transfers between devices: 227 us -> none  [the longest x2 227 us: combined_all(): gathered = jax.tree.map(lambda a: lax.all_gather(a, axis), part)]
    dot_general x12 -> x0, matrix products: 142 us -> none  [cross_costs(): lax.dot_general(piece, right, (((0,), (0,)), ((), ())), precision=lax.Pre...]
    pmax x2 -> x0, blocking collectives: 70.2 us -> none  [row_lse(): best = lax.pmax(tops, 'col')]
    pallas_call x0 -> x1, Pallas kernels: none -> 69.7 us  [body(): pl.pallas_call(kernel, out_shape=(jax.ShapeDtypeStruct((1, XB), F32), jax...]
    dynamic_slice x85 -> x0, local copies, waits for them, and re-layouts: 65.9 us -> none  [the longest x66 63.9 us: take(): lax.dynamic_index_in_dim(a, source, 0, False)]
    reduce_sum x14 -> x0, other arithmetic: 57.3 us -> none  [the longest x8 37.1 us: one(): return (top, jnp.sum(jnp.exp(scores - top[:, None]), 1))]
    psum x2 -> x0, blocking collectives: 12 us -> none  [row_lse(): summed = lax.psum(totals * jnp.exp(tops - best), 'col')]
  transfers between devices with their start and end apart: 3 -> 0, of which waited for: 2 -> 0; matrix products, arithmetic and copies ran while one was open for 0% -> 0% of each run, Pallas kernels for 0% -> 0%
where the time goes in v1:
time: 74.5 us; the launch traced here: 74.3 us
  Pallas kernels  69.7 us (94%)
  local copies, waits for them, and re-layouts  3.91 us (5%)
    pallas_call x1, Pallas kernels, body(): pl.pallas_call(kernel, out_shape=(jax.ShapeDtypeStruct((1, XB), F32), jax...  69.7 us
    unnamed x13, local copies, waits for them, and re-layouts  3.91 us

profile of v1, /device:TPU:1, one launch (start us, length us, event | category | flops | bytes accessed | tf_op | source)
XLA Modules:
  0.0 74.3 jit_solution(13520761483810574897)
XLA Ops:
  0.6 0.0 copy-start.4
  0.6 0.0 copy-start.2
  0.7 0.0 copy-start.3
  0.7 0.6 copy-done.4
  1.3 0.0 copy-done.2
  1.3 0.0 copy-done.3
  1.3 0.0 copy-start
  1.3 0.8 %copy-done = f32[64,256]{1,0:T(8,128)S(1)} copy-done((f32[64,256]{1,0:T(8,128)S(1)}, f32[64,256]{1,0:T(8,128)}, u32[]{:S(2)}) %copy-start) | copy-done | bytes 65560
  2.2 0.0 copy-start.1
  2.2 0.8 %copy-done.1 = f32[64,128]{1,0:T(8,128)S(1)} copy-done((f32[64,128]{1,0:T(8,128)S(1)}, f32[64,128]{1,0:T(8,128)}, u32[]{:S(2)}) %copy-start.1) | copy-done | bytes 32792
  2.9 69.7 %shard_map.76 = (f32[1,256]{1,0:T(1,128)S(1)}, f32[1,128]{1,0:T(1,128)S(1)}, f32[1,256]{1,0:T(1,128)S(1)}) custom-call(f32[64,256]{1,0:T(8,128)S(1)} %copy-done, f32[64,128]{1,0:T(8,128)S(1)} %copy-done.1, f32[1,128]{1,0:T(1,128)S(1)} %bitcast.9, f32[1,256]{1,0:T(1,128)S(1)} %bitcast.6, f32[1,128]{1,0:T(1,128)S(1)} %bitcast.10), custom_call_target="tpu_custom_call" | custom-call | tf_op jit(solution)/shard_map/pallas_call | solution.py:375
  72.6 0.6 copy.11
  73.2 0.5 copy.12
  73.7 0.6 copy.13
Async XLA Ops:
  0.6 0.7 copy-start.4
  0.6 0.7 copy-start.2
  0.7 0.7 copy-start.3
  1.3 0.8 %copy-start = (f32[64,256]{1,0:T(8,128)S(1)}, f32[64,256]{1,0:T(8,128)}, u32[]{:S(2)}) copy-start(f32[64,256]{1,0:T(8,128)} %measured.1) | copy-start | bytes 196612
  2.2 0.8 %copy-start.1 = (f32[64,128]{1,0:T(8,128)S(1)}, f32[64,128]{1,0:T(8,128)}, u32[]{:S(2)}) copy-start(f32[64,128]{1,0:T(8,128)} %generated.1) | copy-start | bytes 98308

commit v2 on v1

v2 whole, which is shorter than its diff:
```python
import functools
import math

import jax
import jax.numpy as jnp
from jax import lax
from jax.experimental import pallas as pl
from jax.experimental.pallas import tpu as pltpu
from jax.sharding import PartitionSpec as P

EPSILON = 0.1
LOG2E = 1.0 / math.log(2.0)
LN2 = math.log(2.0)
MESH = pl.DeviceIdType.MESH
F32 = jnp.float32
BF16 = jnp.bfloat16

GRID = {"z": 8, "y": 4, "xh": 2, "xl": 2}
XB = 256
YB = 128
DIM = 64


def kernel(
    measured_hbm,
    generated_hbm,
    previous_hbm,
    row_weight_hbm,
    col_weight_hbm,
    row_out,
    col_out,
    gap_out,
    measured,
    generated,
    previous,
    row_weight,
    col_weight,
    xraw,
    yraw,
    yt,
    xaug,
    cstat,
    sstat,
    row_stat_out,
    row_stat_in,
    rbuf,
    rfull,
    col_stat_out,
    col_stat_in,
    qbuf,
    w_out,
    w_in,
    in_sem,
    x_send,
    x_recv,
    y_send,
    y_recv,
    row_send,
    row_recv,
    r_send,
    r_recv,
    col_send,
    col_recv,
    q_send,
    q_recv,
    w_send,
    w_recv,
    *scores,
):
    NZ, NY, NXH, NXL = GRID["z"], GRID["y"], GRID["xh"], GRID["xl"]
    NX = NXH * NXL
    NQ, NP = NX * NY, NZ * 2
    NI = NQ * XB
    NL = NI // 128
    ndev = NQ * NP

    loads = [
        pltpu.make_async_copy(src, dst, in_sem.at[n])
        for n, (src, dst) in enumerate(
            [
                (generated_hbm, generated),
                (previous_hbm, previous),
                (col_weight_hbm, col_weight),
                (measured_hbm, measured),
                (row_weight_hbm, row_weight),
            ]
        )
    ]
    for c in loads:
        c.start()

    row = lax.axis_index("row")
    col = lax.axis_index("col")
    z = row // (NY * NXH)
    y = (row // NXH) % NY
    x = (row % NXH) * NXL + col // 2
    core = col % 2

    def device(dz, dy, dx, dc):
        zz, yy, xx = (z + dz) % NZ, (y + dy) % NY, (x + dx) % NX
        return ((zz * NY + yy) * NXH + xx // NXL, (xx % NXL) * 2 + (core + dc) % 2)

    def xslot(dy, dx):
        return (dy % NY) * NX + dx % NX

    def yslot(dz, dc):
        return (dz % NZ) * 2 + dc % 2

    def copy(src, dst, send, recv, dev):
        return pltpu.make_async_remote_copy(
            src_ref=src, dst_ref=dst, send_sem=send, recv_sem=recv, device_id=dev, device_id_type=MESH
        )

    def near_first(n):
        return sorted(range(1, n), key=lambda d: min(d, n - d))

    plane = [(dy, dx) for dy in range(NY) for dx in range(NX) if (dy, dx) != (0, 0)]
    line = [(dz, dc) for dz in range(NZ) for dc in range(2) if (dz, dc) != (0, 0)]

    barrier = pltpu.get_barrier_semaphore()
    for dy, dx in plane:
        pl.semaphore_signal(barrier, inc=1, device_id=device(0, dy, dx, 0), device_id_type=MESH)
    for dz, dc in line:
        pl.semaphore_signal(barrier, inc=1, device_id=device(dz, 0, 0, dc), device_id_type=MESH)

    for c in loads:
        c.wait()
    scale = 2.0 * LOG2E / EPSILON
    xraw[0] = measured[...] * scale
    gen = generated[...]
    log_b = jnp.log(col_weight[...]) - math.log(YB * ndev)
    ysq = jnp.sum(gen * gen, axis=0, keepdims=True)
    u = (log_b + (previous[...] - ysq) / EPSILON) * LOG2E
    yraw[0, 0:DIM] = gen
    yraw[0, DIM : DIM + 8] = jnp.broadcast_to(u, (8, YB))
    log_a = jnp.log(row_weight[...]) - math.log(XB * ndev)
    xsq = jnp.sum(measured[...] * measured[...], axis=0, keepdims=True)
    xaug[:, 3 * DIM :] = jnp.ones((NQ // 2, DIM, 2 * XB), BF16)

    pl.semaphore_wait(barrier, len(plane) + len(line))

    pending = []

    def start(c):
        c.start()
        pending.append(c)

    half = DIM // 2
    counter = [0]

    def send_x(slot, part, dst_slot, dev):
        at = pl.ds(part * half, half)
        n = counter[0]
        counter[0] += 1
        start(copy(xraw.at[slot, at], xraw.at[dst_slot, at], x_send.at[n], x_recv.at[dst_slot, part], dev))

    def wait_x(slot, part):
        at = pl.ds(part * half, half)
        copy(xraw.at[slot, at], xraw.at[slot, at], x_send.at[0], x_recv.at[slot, part], device(0, 0, 1, 0)).wait_recv()

    def send_y(n, slot, dst_slot, dev):
        start(copy(yraw.at[slot], yraw.at[dst_slot], y_send.at[n], y_recv.at[dst_slot], dev))

    def wait_y(slot):
        copy(yraw.at[slot], yraw.at[slot], y_send.at[0], y_recv.at[slot], device(0, 0, 0, 1)).wait_recv()

    for ez in near_first(NZ):
        send_y(ez, 0, yslot(-ez, 0), device(ez, 0, 0, 0))
    send_y(0, 0, yslot(0, 1), device(0, 0, 0, 1))
    for part in range(2):
        for e in near_first(max(NX, NY)):
            if e < NX:
                send_x(0, part, xslot(0, -e), device(0, 0, e, 0))
            if e < NY:
                send_x(0, 1 - part, xslot(-e, 0), device(0, e, 0, 0))

    def forward_x(d):
        if d < NX:
            wait_x(xslot(0, d), 0)
            for ey in near_first(NY):
                send_x(xslot(0, d), 0, xslot(-ey, d), device(0, ey, 0, 0))
        if d < NY:
            wait_x(xslot(d, 0), 1)
            for ex in near_first(NX):
                send_x(xslot(d, 0), 1, xslot(d, -ex), device(0, 0, ex, 0))

    def forward_y(dz):
        wait_y(yslot(dz, 0))
        send_y(NZ + dz, yslot(dz, 0), yslot(dz, 1), device(0, 0, 0, 1))

    def split(v):
        hi = v.astype(BF16).astype(F32)
        return hi, v - hi

    sub128 = lax.broadcasted_iota(jnp.int32, (8, YB), 0)

    def turn_y(slot):
        hi, lo = split(yraw[slot, 0:DIM])
        t1, rest = split(yraw[slot, DIM : DIM + 8])
        t2, t3 = split(rest)
        extra = jnp.where(sub128 == 0, t1, jnp.where(sub128 == 1, t2, jnp.where(sub128 == 2, t3, 0.0)))
        at = slice(slot * YB, (slot + 1) * YB)
        yt[at, 0 : 2 * DIM] = jnp.concatenate([hi, hi], axis=0).T.astype(BF16)
        yt[at, 2 * DIM :] = jnp.concatenate([lo, extra, jnp.zeros((DIM - 8, YB), F32)], axis=0).T.astype(BF16)

    def take_x(slot):
        v = xraw[slot]
        hi = v.astype(BF16)
        lo = (v - hi.astype(F32)).astype(BF16)
        at = slice((slot % 2) * XB, (slot % 2 + 1) * XB)
        xaug[slot // 2, 0:DIM, at] = hi
        xaug[slot // 2, DIM : 2 * DIM, at] = lo
        xaug[slot // 2, 2 * DIM : 3 * DIM, at] = hi

    waited = set()

    def ready_x(pair):
        for slot in (2 * pair, 2 * pair + 1):
            dy, dx = slot // NX, slot % NX
            for part in range(2):
                if slot > 0 and not (dy == 0 and part == 0) and not (dx == 0 and part == 1):
                    wait_x(slot, part)
            take_x(slot)

    CH = 2 * YB
    PW = 2 * XB

    def dot_stage(pair, c):
        scores[pair][c * CH : (c + 1) * CH] = jnp.dot(
            yt[c * CH : (c + 1) * CH], xaug[pair], preferred_element_type=F32
        )

    def rows8(pair, c, k):
        return scores[pair][c * CH + k * 8 : c * CH + (k + 1) * 8]

    def max_stage(pair, c, accs):
        accs = list(accs)
        for k in range(CH // 8):
            accs[k % 2] = jnp.maximum(accs[k % 2], rows8(pair, c, k))
        return accs

    def exp_stage(pair, c, top, accs):
        accs = list(accs)
        for k in range(CH // 8):
            accs[k % 2] = accs[k % 2] + jnp.exp2(rows8(pair, c, k) - top)
        return accs

    def finish_rows(pair, top, total):
        best = jnp.max(top, axis=0, keepdims=True)
        summed = jnp.sum(total * jnp.exp2(top - best), axis=0, keepdims=True)
        for h in range(2):
            slot = 2 * pair + h
            ref = row_stat_in if slot == 0 else row_stat_out
            ref[slot, :, 0:XB] = best[:, h * XB : (h + 1) * XB]
            ref[slot, :, XB:] = summed[:, h * XB : (h + 1) * XB]

    def send_rows(pair):
        for slot in (2 * pair, 2 * pair + 1):
            if slot > 0:
                dy, dx = slot // NX, slot % NX
                dst = xslot(-dy, -dx)
                copy(
                    row_stat_out.at[slot], row_stat_in.at[dst], row_send.at[slot], row_recv.at[dst], device(0, dy, dx, 0)
                ).start()

    for d in near_first(max(NX, NY))[:2]:
        forward_x(d)
    turn_y(0)
    order = [0] + near_first(NZ)
    late = near_first(max(NX, NY))[2:]
    lag = 2
    for n in range(NZ + lag):
        if 0 < n < NZ:
            forward_y(order[n])
            turn_y(yslot(order[n], 0))
        if n == 2:
            for d in late:
                forward_x(d)
            ready_x(0)
        if n >= lag:
            dz = order[n - lag]
            wait_y(yslot(dz, 1))
            turn_y(yslot(dz, 1))
            dot_stage(0, dz)

    near = lambda dy: min(dy, NY - dy)
    pairs = sorted(range(NQ // 2), key=lambda p: (near(2 * p // NX), p))
    state = {}
    for step in range(1, len(pairs) + 3):
        one = pairs[step] if step < len(pairs) else None
        two = pairs[step - 1] if 0 <= step - 1 < len(pairs) else None
        three = pairs[step - 2] if 0 <= step - 2 < len(pairs) else None
        if step >= 4:
            send_rows(pairs[step - 4])
        if one is not None:
            ready_x(one)
        tops = [jnp.full((8, PW), -3e38, F32)] * 2
        sums = [jnp.zeros((8, PW), F32)] * 2
        for c in range(NZ):
            if one is not None:
                dot_stage(one, c)
            if two is not None:
                tops = max_stage(two, c, tops)
            if three is not None:
                sums = exp_stage(three, c, state[three], sums)
        if step >= 3 and step - 3 < len(pairs):
            finish_rows(*state.pop("done"))
        if two is not None:
            state[two] = jnp.maximum(*tops)
        if three is not None:
            state["done"] = (three, state.pop(three), sums[0] + sums[1])
    send_rows(pairs[-1])

    def wait_in(buf, slot, send, recv):
        copy(buf.at[slot], buf.at[slot], send.at[slot], recv.at[slot], device(0, 0, 1, 0)).wait_recv()

    def wait_out(buf, slot, send, recv):
        copy(buf.at[slot], buf.at[slot], send.at[slot], recv.at[slot], device(0, 0, 1, 0)).wait_send()

    for k in range(1, NQ):
        wait_in(row_stat_in, k, row_send, row_recv)

    def combined(ref, n, width):
        tops = [ref[k, :, 0:width] for k in range(n)]
        best = functools.reduce(jnp.maximum, tops)
        summed = functools.reduce(jnp.add, [ref[k, :, width:] * jnp.exp2(tops[k] - best) for k in range(n)])
        return best + jnp.log(summed) * LOG2E

    row_lse = combined(row_stat_in, NQ, XB)
    rbuf[0] = log_a * LOG2E - row_lse
    for dy, dx in plane:
        s, d = xslot(dy, dx), xslot(-dy, -dx)
        copy(rbuf.at[0], rbuf.at[d], r_send.at[s], r_recv.at[d], device(0, dy, dx, 0)).start()
    row_out[...] = xsq - (EPSILON * LN2) * row_lse
    for k in range(1, NQ):
        wait_in(rbuf, k, r_send, r_recv)
    for k in range(NQ):
        rfull[:, k * XB : (k + 1) * XB] = jnp.broadcast_to(rbuf[k], (8, XB))

    eye = lax.broadcasted_iota(jnp.int32, (YB, YB), 0) == lax.broadcasted_iota(jnp.int32, (YB, YB), 1)
    per = PW // 128

    def across(v):
        return jnp.sum(jnp.where(eye, v, 0.0), axis=0, keepdims=True)

    def rows_of(b):
        return pl.ds(pl.multiple_of(b * YB, YB), YB)

    def col_tiles(b):
        at = rows_of(b)
        blocks = [s.at[at] for s in scores]
        cblock, sblock = cstat.at[at], sstat.at[at]
        for t in range(YB // 8):
            r8 = slice(t * 8, (t + 1) * 8)
            vals = [
                blocks[l // per][r8, (l % per) * 128 : (l % per + 1) * 128] + rfull[:, l * 128 : (l + 1) * 128]
                for l in range(NL)
            ]
            tops = vals
            while len(tops) > 1:
                tops = [jnp.maximum(tops[i], tops[i + 1]) for i in range(0, len(tops), 2)]
            top = tops[0]
            parts = [None] * 4
            for l in range(NL):
                p = jnp.exp2(vals[l] - top)
                blocks[l // per][r8, (l % per) * 128 : (l % per + 1) * 128] = p
                parts[l % 4] = p if l < 4 else parts[l % 4] + p
            cblock[r8] = top
            sblock[r8] = (parts[0] + parts[1]) + (parts[2] + parts[3])

    def col_stats(b):
        c = cstat[rows_of(b), :]
        best = jnp.max(c, axis=1, keepdims=True)
        summed = jnp.sum(sstat[rows_of(b), :] * jnp.exp2(c - best), axis=1, keepdims=True)
        return across(best), across(summed)

    def put_stats(ref, b, stats):
        ref[b, :, 0:YB] = stats[0]
        ref[b, :, YB:] = stats[1]

    def send_cols(b):
        dz, dc = b // 2, b % 2
        dst = ((NZ - dz) % NZ) * 2 + dc
        copy(col_stat_out.at[b], col_stat_in.at[dst], col_send.at[b], col_recv.at[dst], device(dz, 0, 0, dc)).start()

    def col_loop(b, carry):
        put_stats(col_stat_out, b - 1, col_stats(b - 1))
        col_tiles(b)
        send_cols(b - 1)
        return carry

    col_tiles(1)
    lax.fori_loop(2, NP, col_loop, 0)
    put_stats(col_stat_out, NP - 1, col_stats(NP - 1))
    col_tiles(0)
    send_cols(NP - 1)
    put_stats(col_stat_in, 0, col_stats(0))
    for k in range(1, NP):
        wait_in(col_stat_in, k, col_send, col_recv)
    col_lse = combined(col_stat_in, NP, YB)
    qbuf[0] = log_b * LOG2E - col_lse
    for dz, dc in line:
        s, d = yslot(dz, dc), yslot(-dz, dc)
        copy(qbuf.at[0], qbuf.at[d], q_send.at[s], q_recv.at[d], device(dz, 0, 0, dc)).start()
    col_out[...] = previous[...] + EPSILON * log_b - (EPSILON * LN2) * col_lse

    for b in range(NP):
        if b > 0:
            wait_in(qbuf, b, q_send, q_recv)
        at = slice(b * YB, (b + 1) * YB)
        cstat[at] = jnp.exp2(cstat[at] + jnp.sum(jnp.where(eye, qbuf[b], 0.0), axis=1, keepdims=True))

    def gap_loop(b, acc):
        at = rows_of(b)
        blocks = [s.at[at] for s in scores]
        gblock = cstat.at[at]
        for t in range(YB // 8):
            r8 = slice(t * 8, (t + 1) * 8)
            g = gblock[r8]
            acc = [acc[l] + blocks[l // per][r8, (l % per) * 128 : (l % per + 1) * 128] * g for l in range(NL)]
        return acc

    acc = lax.fori_loop(0, NP, gap_loop, [jnp.zeros((8, 128), F32) for _ in range(NL)])
    for k in range(NQ):
        for h in range(2):
            ref = w_in if k == 0 else w_out
            ref[k, :, h * 128 : (h + 1) * 128] = jnp.sum(acc[2 * k + h], axis=0, keepdims=True)
    for dy, dx in plane:
        s, d = xslot(dy, dx), xslot(-dy, -dx)
        copy(w_out.at[s], w_in.at[d], w_send.at[s], w_recv.at[d], device(0, dy, dx, 0)).start()

    for c in pending:
        c.wait_send()
    for k in range(1, NQ):
        wait_out(row_stat_out, k, row_send, row_recv)
        wait_out(rbuf, k, r_send, r_recv)
    for k in range(1, NP):
        wait_out(col_stat_out, k, col_send, col_recv)
        wait_out(qbuf, k, q_send, q_recv)

    for k in range(1, NQ):
        wait_in(w_in, k, w_send, w_recv)
    mass = functools.reduce(jnp.add, [w_in[k] for k in range(NQ)])
    gap_out[...] = jnp.log(mass) - log_a
    for k in range(1, NQ):
        wait_out(w_out, k, w_send, w_recv)


def body(measured, generated, previous, row_weight, col_weight):
    NQ = GRID["y"] * GRID["xh"] * GRID["xl"]
    NP = GRID["z"] * 2
    NJ, NI = NP * YB, NQ * XB
    dma = pltpu.SemaphoreType.DMA
    row, col, gap = pl.pallas_call(
        kernel,
        out_shape=(
            jax.ShapeDtypeStruct((1, XB), F32),
            jax.ShapeDtypeStruct((1, YB), F32),
            jax.ShapeDtypeStruct((1, XB), F32),
        ),
        in_specs=[pl.BlockSpec(memory_space=pltpu.HBM)] * 5,
        out_specs=(pl.BlockSpec(memory_space=pltpu.VMEM),) * 3,
        scratch_shapes=[
            pltpu.VMEM((DIM, XB), F32),
            pltpu.VMEM((DIM, YB), F32),
            pltpu.VMEM((1, YB), F32),
            pltpu.VMEM((1, XB), F32),
            pltpu.VMEM((1, YB), F32),
            pltpu.VMEM((NQ, DIM, XB), F32),
            pltpu.VMEM((NP, DIM + 8, YB), F32),
            pltpu.VMEM((NJ, 4 * DIM), BF16),
            pltpu.VMEM((NQ // 2, 4 * DIM, 2 * XB), BF16),
            pltpu.VMEM((NJ, 128), F32),
            pltpu.VMEM((NJ, 128), F32),
            pltpu.VMEM((NQ, 1, 2 * XB), F32),
            pltpu.VMEM((NQ, 1, 2 * XB), F32),
            pltpu.VMEM((NQ, 1, XB), F32),
            pltpu.VMEM((8, NI), F32),
            pltpu.VMEM((NP, 1, 2 * YB), F32),
            pltpu.VMEM((NP, 1, 2 * YB), F32),
            pltpu.VMEM((NP, 1, YB), F32),
            pltpu.VMEM((NQ, 1, XB), F32),
            pltpu.VMEM((NQ, 1, XB), F32),
            dma((5,)),
            dma((2 * NQ,)),
            dma((NQ, 2)),
            dma((NP,)),
            dma((NP,)),
            dma((NQ,)),
            dma((NQ,)),
            dma((NQ,)),
            dma((NQ,)),
            dma((NP,)),
            dma((NP,)),
            dma((NP,)),
            dma((NP,)),
            dma((NQ,)),
            dma((NQ,)),
            *[pltpu.VMEM((NJ, 2 * XB), F32) for _ in range(NQ // 2)],
        ],
        compiler_params=pltpu.CompilerParams(
            collective_id=0, has_side_effects=True, vmem_limit_bytes=48 * 1024 * 1024
        ),
    )(
        measured,
        generated,
        previous.reshape(1, YB),
        row_weight.reshape(1, XB),
        col_weight.reshape(1, YB),
    )
    return row.reshape(XB), col.reshape(YB), gap.reshape(XB)


def solution(mesh):
    placed = (
        P(None, ("row", "col")),
        P(None, ("col", "row")),
        P(("col", "row")),
        P(("row", "col")),
        P(("col", "row")),
    )
    return jax.shard_map(
        body,
        mesh=mesh,
        in_specs=placed,
        out_specs=(P(("row", "col")), P(("col", "row")), P(("row", "col"))),
        check_vma=False,
    )
```

time: 74.5 us -> 70.5 us (0.946)
  Pallas kernels: 69.7 us -> 65.8 us
    pallas_call x1, Pallas kernels: 69.7 us -> 65.8 us  [body(): pl.pallas_call(kernel, out_shape=(jax.ShapeDtypeStruct((1, XB), F32), jax...]
where the time goes in v2:
time: 70.5 us; the launch traced here: 70.3 us
  Pallas kernels  65.8 us (93%)
  local copies, waits for them, and re-layouts  3.91 us (6%)
    pallas_call x1, Pallas kernels, body(): pl.pallas_call(kernel, out_shape=(jax.ShapeDtypeStruct((1, XB), F32), jax...  65.8 us
    unnamed x13, local copies, waits for them, and re-layouts  3.91 us

profile of v2, /device:TPU:1, one launch (start us, length us, event | category | flops | bytes accessed | tf_op | source)
XLA Modules:
  0.0 70.3 jit_solution(950369654004432078)
XLA Ops:
  0.6 0.0 copy-start.4
  0.6 0.0 copy-start.2
  0.7 0.0 copy-start.3
  0.7 0.6 copy-done.4
  1.3 0.0 copy-done.2
  1.3 0.0 copy-done.3
  1.3 0.0 copy-start
  1.3 0.8 %copy-done = f32[64,256]{1,0:T(8,128)S(1)} copy-done((f32[64,256]{1,0:T(8,128)S(1)}, f32[64,256]{1,0:T(8,128)}, u32[]{:S(2)}) %copy-start) | copy-done | bytes 65560
  2.2 0.0 copy-start.1
  2.2 0.8 %copy-done.1 = f32[64,128]{1,0:T(8,128)S(1)} copy-done((f32[64,128]{1,0:T(8,128)S(1)}, f32[64,128]{1,0:T(8,128)}, u32[]{:S(2)}) %copy-start.1) | copy-done | bytes 32792
  2.9 65.8 %shard_map.76 = (f32[1,256]{1,0:T(1,128)S(1)}, f32[1,128]{1,0:T(1,128)S(1)}, f32[1,256]{1,0:T(1,128)S(1)}) custom-call(f32[64,256]{1,0:T(8,128)S(1)} %copy-done, f32[64,128]{1,0:T(8,128)S(1)} %copy-done.1, f32[1,128]{1,0:T(1,128)S(1)} %bitcast.9, f32[1,256]{1,0:T(1,128)S(1)} %bitcast.6, f32[1,128]{1,0:T(1,128)S(1)} %bitcast.10), custom_call_target="tpu_custom_call" | custom-call | tf_op jit(solution)/shard_map/pallas_call | solution.py:454
  68.7 0.6 copy.11
  69.3 0.5 copy.12
  69.8 0.6 copy.13
Async XLA Ops:
  0.6 0.7 copy-start.4
  0.6 0.7 copy-start.2
  0.7 0.7 copy-start.3
  1.3 0.8 %copy-start = (f32[64,256]{1,0:T(8,128)S(1)}, f32[64,256]{1,0:T(8,128)}, u32[]{:S(2)}) copy-start(f32[64,256]{1,0:T(8,128)} %measured_hbm.1) | copy-start | bytes 196612
  2.2 0.8 %copy-start.1 = (f32[64,128]{1,0:T(8,128)S(1)}, f32[64,128]{1,0:T(8,128)}, u32[]{:S(2)}) copy-start(f32[64,128]{1,0:T(8,128)} %generated_hbm.1) | copy-start | bytes 98308

commit v3 on v2

--- a/solution.py
+++ b/solution.py
@@ -19,6 +19,7 @@
 XB = 256
 YB = 128
 DIM = 64
+QUARTERS = 4
 
 
 def kernel(
@@ -65,7 +66,7 @@
     q_recv,
     w_send,
     w_recv,
-    *scores,
+    *parts,
 ):
     NZ, NY, NXH, NXL = GRID["z"], GRID["y"], GRID["xh"], GRID["xl"]
     NX = NXH * NXL
@@ -73,6 +74,9 @@
     NI = NQ * XB
     NL = NI // 128
     ndev = NQ * NP
+
+    QR = NP * YB // QUARTERS
+    quarter = [parts[h * (NQ // 2) : (h + 1) * (NQ // 2)] for h in range(QUARTERS + 1)]
 
     loads = [
         pltpu.make_async_copy(src, dst, in_sem.at[n])
@@ -226,12 +230,16 @@
     PW = 2 * XB
 
     def dot_stage(pair, c):
-        scores[pair][c * CH : (c + 1) * CH] = jnp.dot(
-            yt[c * CH : (c + 1) * CH], xaug[pair], preferred_element_type=F32
-        )
+        for n in range(max(1, CH // QR)):
+            size = min(CH, QR)
+            r = c * CH + n * size
+            quarter[r // QR][pair][r % QR : r % QR + size] = jnp.dot(
+                yt[r : r + size], xaug[pair], preferred_element_type=F32
+            )
 
     def rows8(pair, c, k):
-        return scores[pair][c * CH + k * 8 : c * CH + (k + 1) * 8]
+        r = c * CH + k * 8
+        return quarter[r // QR][pair][r % QR : r % QR + 8]
 
     def max_stage(pair, c, accs):
         accs = list(accs)
@@ -346,10 +354,15 @@
     def rows_of(b):
         return pl.ds(pl.multiple_of(b * YB, YB), YB)
 
-    def col_tiles(b):
-        at = rows_of(b)
-        blocks = [s.at[at] for s in scores]
-        cblock, sblock = cstat.at[at], sstat.at[at]
+    BQ = QR // YB
+
+    def tiles_of(h, b):
+        at = pl.ds(pl.multiple_of((b - h * BQ) * YB, YB), YB)
+        return [s.at[at] for s in quarter[h]]
+
+    def col_tiles(h, b):
+        blocks, puts = tiles_of(h, b), [s.at[pl.ds(pl.multiple_of((b - h * BQ) * YB, YB), YB)] for s in quarter[h - 1]]
+        cblock, sblock = cstat.at[rows_of(b)], sstat.at[rows_of(b)]
         for t in range(YB // 8):
             r8 = slice(t * 8, (t + 1) * 8)
             vals = [
@@ -360,13 +373,13 @@
             while len(tops) > 1:
                 tops = [jnp.maximum(tops[i], tops[i + 1]) for i in range(0, len(tops), 2)]
             top = tops[0]
-            parts = [None] * 4
+            sums = [None] * 4
             for l in range(NL):
-                p = jnp.exp2(vals[l] - top)
-                blocks[l // per][r8, (l % per) * 128 : (l % per + 1) * 128] = p
-                parts[l % 4] = p if l < 4 else parts[l % 4] + p
+                e = jnp.exp2(vals[l] - top)
+                puts[l // per][r8, (l % per) * 128 : (l % per + 1) * 128] = e
+                sums[l % 4] = e if l < 4 else sums[l % 4] + e
             cblock[r8] = top
-            sblock[r8] = (parts[0] + parts[1]) + (parts[2] + parts[3])
+            sblock[r8] = (sums[0] + sums[1]) + (sums[2] + sums[3])
 
     def col_stats(b):
         c = cstat[rows_of(b), :]
@@ -383,18 +396,28 @@
         dst = ((NZ - dz) % NZ) * 2 + dc
         copy(col_stat_out.at[b], col_stat_in.at[dst], col_send.at[b], col_recv.at[dst], device(dz, 0, 0, dc)).start()
 
-    def col_loop(b, carry):
-        put_stats(col_stat_out, b - 1, col_stats(b - 1))
-        col_tiles(b)
-        send_cols(b - 1)
-        return carry
-
-    col_tiles(1)
-    lax.fori_loop(2, NP, col_loop, 0)
+    def col_loop(h):
+        def step(b, carry):
+            put_stats(col_stat_out, b - 1, col_stats(b - 1))
+            col_tiles(h, b)
+            send_cols(b - 1)
+            return carry
+
+        return step
+
+    col_tiles(0, 0)
+    put_stats(col_stat_in, 0, col_stats(0))
+    for h in range(QUARTERS):
+        if h == 0:
+            if BQ > 1:
+                col_tiles(0, 1)
+            lax.fori_loop(2, BQ, col_loop(0), 0)
+        elif h == 1 and BQ == 1:
+            col_tiles(1, 1)
+        else:
+            lax.fori_loop(h * BQ, (h + 1) * BQ, col_loop(h), 0)
     put_stats(col_stat_out, NP - 1, col_stats(NP - 1))
-    col_tiles(0)
     send_cols(NP - 1)
-    put_stats(col_stat_in, 0, col_stats(0))
     for k in range(1, NP):
         wait_in(col_stat_in, k, col_send, col_recv)
     col_lse = combined(col_stat_in, NP, YB)
@@ -410,17 +433,22 @@
         at = slice(b * YB, (b + 1) * YB)
         cstat[at] = jnp.exp2(cstat[at] + jnp.sum(jnp.where(eye, qbuf[b], 0.0), axis=1, keepdims=True))
 
-    def gap_loop(b, acc):
-        at = rows_of(b)
-        blocks = [s.at[at] for s in scores]
-        gblock = cstat.at[at]
-        for t in range(YB // 8):
-            r8 = slice(t * 8, (t + 1) * 8)
-            g = gblock[r8]
-            acc = [acc[l] + blocks[l // per][r8, (l % per) * 128 : (l % per + 1) * 128] * g for l in range(NL)]
-        return acc
-
-    acc = lax.fori_loop(0, NP, gap_loop, [jnp.zeros((8, 128), F32) for _ in range(NL)])
+    def gap_loop(h):
+        def step(b, acc):
+            at = pl.ds(pl.multiple_of((b - h * BQ) * YB, YB), YB)
+            blocks = [s.at[at] for s in quarter[h - 1]]
+            gblock = cstat.at[rows_of(b)]
+            for t in range(YB // 8):
+                r8 = slice(t * 8, (t + 1) * 8)
+                g = gblock[r8]
+                acc = [acc[l] + blocks[l // per][r8, (l % per) * 128 : (l % per + 1) * 128] * g for l in range(NL)]
+            return acc
+
+        return step
+
+    acc = [jnp.zeros((8, 128), F32) for _ in range(NL)]
+    for h in range(QUARTERS):
+        acc = lax.fori_loop(h * BQ, (h + 1) * BQ, gap_loop(h), acc)
     for k in range(NQ):
         for h in range(2):
             ref = w_in if k == 0 else w_out
@@ -444,6 +472,17 @@
     gap_out[...] = jnp.log(mass) - log_a
     for k in range(1, NQ):
         wait_out(w_out, k, w_send, w_recv)
+
+
+def put_results(row, col, gap, row_out, col_out, gap_out, sem):
+    copies = [
+        pltpu.make_async_copy(src, dst, sem.at[n])
+        for n, (src, dst) in enumerate([(row, row_out), (col, col_out), (gap, gap_out)])
+    ]
+    for c in copies:
+        c.start()
+    for c in copies:
+        c.wait()
 
 
 def body(measured, generated, previous, row_weight, col_weight):
@@ -496,18 +535,35 @@
             dma((NP,)),
             dma((NQ,)),
             dma((NQ,)),
-            *[pltpu.VMEM((NJ, 2 * XB), F32) for _ in range(NQ // 2)],
+            *[pltpu.VMEM((NJ // QUARTERS, 2 * XB), F32) for _ in range((QUARTERS + 1) * (NQ // 2))],
         ],
         compiler_params=pltpu.CompilerParams(
-            collective_id=0, has_side_effects=True, vmem_limit_bytes=48 * 1024 * 1024
+            collective_id=0, has_side_effects=True, vmem_limit_bytes=50 * 1024 * 1024
         ),
     )(
-        measured,
-        generated,
-        previous.reshape(1, YB),
-        row_weight.reshape(1, XB),
-        col_weight.reshape(1, YB),
+        *[
+            pltpu.with_memory_space_constraint(v, pltpu.HBM)
+            for v in (
+                measured,
+                generated,
+                previous.reshape(1, YB),
+                row_weight.reshape(1, XB),
+                col_weight.reshape(1, YB),
+            )
+        ]
     )
+    row, col, gap = pl.pallas_call(
+        put_results,
+        out_shape=(
+            jax.ShapeDtypeStruct((1, XB), F32),
+            jax.ShapeDtypeStruct((1, YB), F32),
+            jax.ShapeDtypeStruct((1, XB), F32),
+        ),
+        in_specs=[pl.BlockSpec(memory_space=pltpu.VMEM)] * 3,
+        out_specs=(pl.BlockSpec(memory_space=pl.ANY),) * 3,
+        scratch_shapes=[dma((3,))],
+        compiler_params=pltpu.CompilerParams(vmem_limit_bytes=1024 * 1024),
+    )(row, col, gap)
     return row.reshape(XB), col.reshape(YB), gap.reshape(XB)
 
 

time: 70.5 us -> 67.5 us (0.957)
  local copies, waits for them, and re-layouts: 3.91 us -> 0 us
    unnamed x13 -> x0, local copies, waits for them, and re-layouts: 3.91 us -> none
where the time goes in v3:
time: 67.5 us; the launch traced here: 67.3 us
  Pallas kernels  66.5 us (99%)
  between operations  0.8 us (1%)
    pallas_call x1, Pallas kernels, body(): pl.pallas_call(kernel, out_shape=(jax.ShapeDtypeStruct((1, XB), F32), jax...  65.9 us

profile of v3, /device:TPU:1, one launch (start us, length us, event | category | flops | bytes accessed | tf_op | source)
XLA Modules:
  0.0 67.3 jit_solution(17577225134606437847)
XLA Ops:
  0.6 65.9 %shard_map.76 = (f32[1,256]{1,0:T(1,128)S(1)}, f32[1,128]{1,0:T(1,128)S(1)}, f32[1,256]{1,0:T(1,128)S(1)}) custom-call(f32[64,256]{1,0:T(8,128)} %measured_hbm.1, f32[64,128]{1,0:T(8,128)} %generated_hbm.1, f32[1,128]{1,0:T(1,128)} %bitcast.7, f32[1,256]{1,0:T(1,128)} %bitcast.6, f32[1,128]{1,0:T(1,128)} %bitcast.8), custom_call_target="tpu_custom_call" | custom-call | tf_op jit(solution)/shard_map/pallas_call | solution.py:493
  66.6 0.6 shard_map.77

commit v4 on v3

--- a/solution.py
+++ b/solution.py
@@ -20,6 +20,30 @@
 YB = 128
 DIM = 64
 QUARTERS = 4
+
+
+ROOT = (
+    0.9999999403953552,
+    0.010830347426235676,
+    5.863578917342238e-05,
+    2.108754131313617e-07,
+    5.476839537443823e-10,
+    8.743147807306617e-13,
+)
+
+
+def power(x):
+    x = jnp.maximum(x, -64.0)
+    p = jnp.full_like(x, ROOT[-1])
+    for c in ROOT[-2::-1]:
+        p = p * x + c
+    for _ in range(6):
+        p = p * p
+    return p
+
+
+def exp2(x, n):
+    return power(x) if n % 8 in (1, 4, 6) else jnp.exp2(x)
 
 
 def kernel(
@@ -250,7 +274,7 @@
     def exp_stage(pair, c, top, accs):
         accs = list(accs)
         for k in range(CH // 8):
-            accs[k % 2] = accs[k % 2] + jnp.exp2(rows8(pair, c, k) - top)
+            accs[k % 2] = accs[k % 2] + exp2(rows8(pair, c, k) - top, k)
         return accs
 
     def finish_rows(pair, top, total):
@@ -375,7 +399,7 @@
             top = tops[0]
             sums = [None] * 4
             for l in range(NL):
-                e = jnp.exp2(vals[l] - top)
+                e = exp2(vals[l] - top, l)
                 puts[l // per][r8, (l % per) * 128 : (l % per + 1) * 128] = e
                 sums[l % 4] = e if l < 4 else sums[l % 4] + e
             cblock[r8] = top

time: 67.5 us -> 79.5 us (1.18)
  Pallas kernels: 66.5 us -> 78.6 us
    pallas_call x1, Pallas kernels: 65.9 us -> 78 us  [body(): pl.pallas_call(kernel, out_shape=(jax.ShapeDtypeStruct((1, XB), F32), jax...]
where the time goes in v4:
time: 79.5 us; the launch traced here: 79.4 us
  Pallas kernels  78.6 us (99%)
  between operations  0.82 us (1%)
    pallas_call x1, Pallas kernels, body(): pl.pallas_call(kernel, out_shape=(jax.ShapeDtypeStruct((1, XB), F32), jax...  78 us

profile of v4, /device:TPU:1, one launch (start us, length us, event | category | flops | bytes accessed | tf_op | source)
XLA Modules:
  0.0 79.4 jit_solution(13486268381265019369)
XLA Ops:
  0.6 78.0 %shard_map.76 = (f32[1,256]{1,0:T(1,128)S(1)}, f32[1,128]{1,0:T(1,128)S(1)}, f32[1,256]{1,0:T(1,128)S(1)}) custom-call(f32[64,256]{1,0:T(8,128)} %measured_hbm.1, f32[64,128]{1,0:T(8,128)} %generated_hbm.1, f32[1,128]{1,0:T(1,128)} %bitcast.7, f32[1,256]{1,0:T(1,128)} %bitcast.6, f32[1,128]{1,0:T(1,128)} %bitcast.8), custom_call_target="tpu_custom_call" | custom-call | tf_op jit(solution)/shard_map/pallas_call | solution.py:517
  78.6 0.6 shard_map.77

commit v5 on v3

v5 whole, which is shorter than its diff:
```python
import functools
import math

import jax
import jax.numpy as jnp
from jax import lax
from jax.experimental import pallas as pl
from jax.experimental.pallas import tpu as pltpu
from jax.sharding import PartitionSpec as P

EPSILON = 0.1
LOG2E = 1.0 / math.log(2.0)
LN2 = math.log(2.0)
MESH = pl.DeviceIdType.MESH
F32 = jnp.float32
BF16 = jnp.bfloat16

GRID = {"z": 8, "y": 4, "xh": 2, "xl": 2}
XB = 256
YB = 128
DIM = 64


def kernel(
    measured_hbm,
    generated_hbm,
    previous_hbm,
    row_weight_hbm,
    col_weight_hbm,
    row_out,
    col_out,
    gap_out,
    measured,
    generated,
    previous,
    row_weight,
    col_weight,
    xraw,
    yraw,
    yt,
    xaug,
    scores,
    row8,
    cstat,
    sstat,
    gbuf,
    row_stat_out,
    row_stat_in,
    rbuf,
    rfull,
    col_stat_out,
    col_stat_in,
    qbuf,
    w_out,
    w_in,
    in_sem,
    x_send,
    x_recv,
    y_send,
    y_recv,
    row_send,
    row_recv,
    r_send,
    r_recv,
    col_send,
    col_recv,
    q_send,
    q_recv,
    w_send,
    w_recv,
):
    NZ, NY, NXH, NXL = GRID["z"], GRID["y"], GRID["xh"], GRID["xl"]
    NX = NXH * NXL
    NQ, NP = NX * NY, NZ * 2
    NI = NQ * XB
    NL = NI // 128
    ndev = NQ * NP

    loads = [
        pltpu.make_async_copy(src, dst, in_sem.at[n])
        for n, (src, dst) in enumerate(
            [
                (generated_hbm, generated),
                (previous_hbm, previous),
                (col_weight_hbm, col_weight),
                (measured_hbm, measured),
                (row_weight_hbm, row_weight),
            ]
        )
    ]
    for c in loads:
        c.start()

    row = lax.axis_index("row")
    col = lax.axis_index("col")
    z = row // (NY * NXH)
    y = (row // NXH) % NY
    x = (row % NXH) * NXL + col // 2
    core = col % 2

    def device(dz, dy, dx, dc):
        zz, yy, xx = (z + dz) % NZ, (y + dy) % NY, (x + dx) % NX
        return ((zz * NY + yy) * NXH + xx // NXL, (xx % NXL) * 2 + (core + dc) % 2)

    def plane(k):
        dy, dx = k // NX, k % NX
        return device(0, dy, dx, 0), ((NY - dy) % NY) * NX + (NX - dx) % NX

    def line(k):
        dz, dc = k // 2, k % 2
        return device(dz, 0, 0, dc), ((NZ - dz) % NZ) * 2 + dc

    def copy(src, dst, send, recv, dev):
        return pltpu.make_async_remote_copy(
            src_ref=src, dst_ref=dst, send_sem=send, recv_sem=recv, device_id=dev, device_id_type=MESH
        )

    def loop(lo, hi, fn):
        def step(k, carry):
            fn(k)
            return carry

        lax.fori_loop(lo, hi, step, 0)

    def near(n, size):
        return (size + (2 * (n % 2) - 1) * ((n + 1) // 2)) % size

    barrier = pltpu.get_barrier_semaphore()
    loop(1, NQ, lambda k: pl.semaphore_signal(barrier, inc=1, device_id=plane(k)[0], device_id_type=MESH))
    loop(1, NP, lambda k: pl.semaphore_signal(barrier, inc=1, device_id=line(k)[0], device_id_type=MESH))

    for c in loads:
        c.wait()
    scale = 2.0 * LOG2E / EPSILON
    xraw[0] = measured[...] * scale
    gen = generated[...]
    log_b = jnp.log(col_weight[...]) - math.log(YB * ndev)
    ysq = jnp.sum(gen * gen, axis=0, keepdims=True)
    u = (log_b + (previous[...] - ysq) / EPSILON) * LOG2E
    yraw[0, 0:DIM] = gen
    yraw[0, DIM : DIM + 8] = jnp.broadcast_to(u, (8, YB))
    log_a = jnp.log(row_weight[...]) - math.log(XB * ndev)
    xsq = jnp.sum(measured[...] * measured[...], axis=0, keepdims=True)
    xaug[:, 3 * DIM :] = jnp.ones((NQ // 2, DIM, 2 * XB), BF16)

    pl.semaphore_wait(barrier, NQ + NP - 2)

    half = DIM // 2

    def x_copy(slot, part, dst_slot, n, dev):
        at = pl.ds(part * half, half)
        return copy(xraw.at[slot, at], xraw.at[dst_slot, at], x_send.at[n], x_recv.at[dst_slot, part], dev)

    def wait_x(slot, part):
        x_copy(slot, part, slot, 0, device(0, 0, 1, 0)).wait_recv()

    def y_copy(n, slot, dst_slot, dev):
        return copy(yraw.at[slot], yraw.at[dst_slot], y_send.at[n], y_recv.at[dst_slot], dev)

    def wait_y(slot):
        y_copy(0, slot, slot, device(0, 0, 0, 1)).wait_recv()

    def send_y(n):
        ez = near(n, NZ)
        y_copy(n, 0, ((NZ - ez) % NZ) * 2, device(ez, 0, 0, 0)).start()

    def send_x(n):
        e = near(n, NX)
        back = (NX - e) % NX
        m = 2 * (n - 1)
        x_copy(0, 0, back, m, device(0, 0, e, 0)).start()
        x_copy(0, 1, back * NX, m + 1, device(0, e, 0, 0)).start()

    def send_x_rest(n):
        e = near(n, NX)
        back = (NX - e) % NX
        m = 2 * (NX - 1) + 2 * (n - 1)
        x_copy(0, 1, back, m, device(0, 0, e, 0)).start()
        x_copy(0, 0, back * NX, m + 1, device(0, e, 0, 0)).start()

    def forward_x(n):
        d = near(n, NX)
        wait_x(d, 0)
        wait_x(d * NX, 1)
        for k in range(1, NX):
            e = near(k, NX)
            back = (NX - e) % NX
            m = 4 * (NX - 1) + 2 * (NX - 1) * (n - 1) + 2 * (k - 1)
            x_copy(d, 0, back * NX + d, m, device(0, e, 0, 0)).start()
            x_copy(d * NX, 1, d * NX + back, m + 1, device(0, 0, e, 0)).start()

    def forward_y(n):
        slot = near(n, NZ) * 2
        wait_y(slot)
        y_copy(NZ + n, slot, slot + 1, device(0, 0, 0, 1)).start()

    y_copy(0, 0, 1, device(0, 0, 0, 1)).start()
    loop(1, NZ, send_y)
    loop(1, NX, send_x)
    loop(1, NX, send_x_rest)

    def split(v):
        hi = v.astype(BF16).astype(F32)
        return hi, v - hi

    sub128 = lax.broadcasted_iota(jnp.int32, (8, YB), 0)

    def turn_y(slot):
        hi, lo = split(yraw[slot, 0:DIM])
        t1, rest = split(yraw[slot, DIM : DIM + 8])
        t2, t3 = split(rest)
        extra = jnp.where(sub128 == 0, t1, jnp.where(sub128 == 1, t2, jnp.where(sub128 == 2, t3, 0.0)))
        at = pl.ds(pl.multiple_of(slot * YB, YB), YB)
        yt[at, 0 : 2 * DIM] = jnp.concatenate([hi, hi], axis=0).T.astype(BF16)
        yt[at, 2 * DIM :] = jnp.concatenate([lo, extra, jnp.zeros((DIM - 8, YB), F32)], axis=0).T.astype(BF16)

    def ready_x(pair):
        dy = pair // (NX // 2)
        for h in range(2):
            dx = (pair % (NX // 2)) * 2 + h

            @pl.when(dy > 0)
            def _():
                wait_x(2 * pair + h, 0)

            @pl.when(dx > 0)
            def _():
                wait_x(2 * pair + h, 1)

        for h in range(2):
            v = xraw[2 * pair + h]
            hi = v.astype(BF16)
            lo = (v - hi.astype(F32)).astype(BF16)
            at = slice(h * XB, (h + 1) * XB)
            xaug[pair, 0:DIM, at] = hi
            xaug[pair, DIM : 2 * DIM, at] = lo
            xaug[pair, 2 * DIM : 3 * DIM, at] = hi

    CH = 2 * YB
    PW = 2 * XB
    NPAIR = NQ // 2

    def rows_at(c):
        return pl.ds(pl.multiple_of(c * CH, CH), CH)

    def dot_stage(pair, c):
        scores[pair, rows_at(c)] = jnp.dot(yt[rows_at(c)], xaug[pair], preferred_element_type=F32)

    def max_stage(pair, c, accs):
        block = scores.at[pair, rows_at(c)]
        accs = list(accs)
        for k in range(CH // 8):
            accs[k % 2] = jnp.maximum(accs[k % 2], block[k * 8 : k * 8 + 8])
        return accs

    def exp_stage(pair, c, top, accs):
        block = scores.at[pair, rows_at(c)]
        accs = list(accs)
        for k in range(CH // 8):
            accs[k % 2] = accs[k % 2] + jnp.exp2(block[k * 8 : k * 8 + 8] - top)
        return accs

    turn_y(0)
    loop(1, NX, forward_x)

    def second_core(n):
        slot = near(n, NZ) * 2 + 1
        wait_y(slot)
        turn_y(slot)
        dot_stage(0, slot // 2)

    def arrive(n):
        forward_y(n)
        slot = near(n, NZ) * 2
        wait_y(near(n - 1, NZ) * 2 + 1)
        turn_y(slot)
        turn_y(near(n - 1, NZ) * 2 + 1)
        dot_stage(0, near(n - 1, NZ))

    forward_y(1)
    ready_x(0)
    turn_y(near(1, NZ) * 2)
    second_core(0)
    loop(2, NZ, arrive)
    second_core(NZ - 1)

    low = jnp.full((8, PW), -3e38, F32)
    zero = jnp.zeros((8, PW), F32)

    def row_step(one, two, three, top):
        def chunk(c, carry):
            tops, sums = carry[:2], carry[2:]
            if three is not None:
                sums = exp_stage(three, c, top, sums)
            if two is not None:
                tops = max_stage(two, c, tops)
            if one is not None:
                dot_stage(one, c)
            return (*tops, *sums)

        out = lax.fori_loop(0, NZ, chunk, (low, low, zero, zero), unroll=2)
        if three is not None:
            row8[three, 0] = top
            row8[three, 1] = out[2] + out[3]
        return jnp.maximum(out[0], out[1])

    def row_loop(step, top):
        ready_x(step)
        return row_step(step, step - 1, step - 2, top)

    ready_x(1)
    top = row_step(1, 0, None, None)
    top = lax.fori_loop(2, NPAIR, row_loop, top)
    top = row_step(None, NPAIR - 1, NPAIR - 2, top)
    row_step(None, None, NPAIR - 1, top)
    for pair in range(NPAIR):
        best = jnp.max(row8[pair, 0], axis=0, keepdims=True)
        summed = jnp.sum(row8[pair, 1] * jnp.exp2(row8[pair, 0] - best), axis=0, keepdims=True)
        for h in range(2):
            slot = 2 * pair + h
            ref = row_stat_in if slot == 0 else row_stat_out
            ref[slot, :, 0:XB] = best[:, h * XB : (h + 1) * XB]
            ref[slot, :, XB:] = summed[:, h * XB : (h + 1) * XB]

    def send_part(src, dst, send, recv, where, k):
        dev, slot = where(k)
        copy(src.at[k], dst.at[slot], send.at[k], recv.at[slot], dev).start()

    def send_all(src, dst, send, recv, where, k):
        dev, slot = where(k)
        copy(src.at[0], dst.at[slot], send.at[k], recv.at[slot], dev).start()

    def wait_in(buf, send, recv, n):
        loop(1, n, lambda k: copy(buf.at[k], buf.at[k], send.at[k], recv.at[k], device(0, 0, 1, 0)).wait_recv())

    def wait_out(buf, send, recv, n):
        loop(1, n, lambda k: copy(buf.at[k], buf.at[k], send.at[k], recv.at[k], device(0, 0, 1, 0)).wait_send())

    def combined(ref, n, width):
        tops = [ref[k, :, 0:width] for k in range(n)]
        best = functools.reduce(jnp.maximum, tops)
        summed = functools.reduce(jnp.add, [ref[k, :, width:] * jnp.exp2(tops[k] - best) for k in range(n)])
        return best + jnp.log(summed) * LOG2E

    loop(1, NQ, lambda k: send_part(row_stat_out, row_stat_in, row_send, row_recv, plane, k))
    wait_in(row_stat_in, row_send, row_recv, NQ)
    row_lse = combined(row_stat_in, NQ, XB)
    rbuf[0] = log_a * LOG2E - row_lse
    loop(1, NQ, lambda k: send_all(rbuf, rbuf, r_send, r_recv, plane, k))
    row_out[...] = xsq - (EPSILON * LN2) * row_lse
    wait_in(rbuf, r_send, r_recv, NQ)
    for k in range(NQ):
        rfull[:, k * XB : (k + 1) * XB] = jnp.broadcast_to(rbuf[k], (8, XB))

    eye = lax.broadcasted_iota(jnp.int32, (YB, YB), 0) == lax.broadcasted_iota(jnp.int32, (YB, YB), 1)
    per = PW // 128

    def across(v):
        return jnp.sum(jnp.where(eye, v, 0.0), axis=0, keepdims=True)

    def rows_of(b):
        return pl.ds(pl.multiple_of(b * YB, YB), YB)

    def lanes(l):
        return slice((l % per) * 128, (l % per + 1) * 128)

    def col_tiles(b):
        blocks = [scores.at[pair, rows_of(b)] for pair in range(NPAIR)]
        cblock, sblock = cstat.at[rows_of(b)], sstat.at[rows_of(b)]
        for t in range(YB // 8):
            r8 = slice(t * 8, (t + 1) * 8)
            vals = [blocks[l // per][r8, lanes(l)] + rfull[:, l * 128 : (l + 1) * 128] for l in range(NL)]
            tops = vals
            while len(tops) > 1:
                tops = [jnp.maximum(tops[i], tops[i + 1]) for i in range(0, len(tops), 2)]
            top = tops[0]
            sums = [None] * 4
            for l in range(NL):
                e = jnp.exp2(vals[l] - top)
                blocks[l // per][r8, lanes(l)] = e
                sums[l % 4] = e if l < 4 else sums[l % 4] + e
            cblock[r8] = top
            sblock[r8] = (sums[0] + sums[1]) + (sums[2] + sums[3])

    def put_stats(b):
        c = cstat[rows_of(b), :]
        best = jnp.max(c, axis=1, keepdims=True)
        summed = jnp.sum(sstat[rows_of(b), :] * jnp.exp2(c - best), axis=1, keepdims=True)
        col_stat_out[b, :, 0:YB] = across(best)
        col_stat_out[b, :, YB:] = across(summed)

    def col_loop(b):
        put_stats(b - 1)
        col_tiles(b)

        @pl.when(b > 1)
        def _():
            send_part(col_stat_out, col_stat_in, col_send, col_recv, line, b - 1)

    col_tiles(0)
    loop(1, NP, col_loop)
    put_stats(NP - 1)
    send_part(col_stat_out, col_stat_in, col_send, col_recv, line, NP - 1)
    col_stat_in[0] = col_stat_out[0]
    wait_in(col_stat_in, col_send, col_recv, NP)
    col_lse = combined(col_stat_in, NP, YB)
    qbuf[0] = log_b * LOG2E - col_lse
    loop(1, NP, lambda k: send_all(qbuf, qbuf, q_send, q_recv, line, k))
    col_out[...] = previous[...] + EPSILON * log_b - (EPSILON * LN2) * col_lse

    def factors(b):
        q = jnp.sum(jnp.where(eye, qbuf[b], 0.0), axis=1, keepdims=True)
        gbuf[b % 2] = jnp.exp2(cstat[rows_of(b), :] + q)

    def gap_loop(b, acc):
        blocks = [scores.at[pair, rows_of(b)] for pair in range(NPAIR)]
        gblock = gbuf.at[b % 2]
        for t in range(YB // 8):
            r8 = slice(t * 8, (t + 1) * 8)
            g = gblock[r8]
            acc = [acc[l] + blocks[l // per][r8, lanes(l)] * g for l in range(NL)]
            if t == YB // 16:
                factors(jnp.minimum(b + 1, NP - 1))
        return acc

    factors(0)
    wait_in(qbuf, q_send, q_recv, NP)
    acc = lax.fori_loop(0, NP, gap_loop, [jnp.zeros((8, 128), F32) for _ in range(NL)])
    for k in range(NQ):
        for h in range(2):
            ref = w_in if k == 0 else w_out
            ref[k, :, h * 128 : (h + 1) * 128] = jnp.sum(acc[2 * k + h], axis=0, keepdims=True)
    loop(1, NQ, lambda k: send_part(w_out, w_in, w_send, w_recv, plane, k))

    loop(0, 2 * NQ - 2, lambda n: x_copy(0, 0, 0, n, device(0, 0, 1, 0)).wait_send())
    loop(0, NZ, lambda n: y_copy(n, 0, 0, device(0, 0, 0, 1)).wait_send())
    loop(NZ + 1, 2 * NZ, lambda n: y_copy(n, 0, 0, device(0, 0, 0, 1)).wait_send())
    wait_out(row_stat_out, row_send, row_recv, NQ)
    wait_out(rbuf, r_send, r_recv, NQ)
    wait_out(col_stat_out, col_send, col_recv, NP)
    wait_out(qbuf, q_send, q_recv, NP)

    wait_in(w_in, w_send, w_recv, NQ)
    mass = functools.reduce(jnp.add, [w_in[k] for k in range(NQ)])
    gap_out[...] = jnp.log(mass) - log_a
    wait_out(w_out, w_send, w_recv, NQ)


def put_results(row, col, gap, row_out, col_out, gap_out, sem):
    copies = [
        pltpu.make_async_copy(src, dst, sem.at[n])
        for n, (src, dst) in enumerate([(row, row_out), (col, col_out), (gap, gap_out)])
    ]
    for c in copies:
        c.start()
    for c in copies:
        c.wait()


def body(measured, generated, previous, row_weight, col_weight):
    NQ = GRID["y"] * GRID["xh"] * GRID["xl"]
    NP = GRID["z"] * 2
    NJ, NI = NP * YB, NQ * XB
    dma = pltpu.SemaphoreType.DMA
    row, col, gap = pl.pallas_call(
        kernel,
        out_shape=(
            jax.ShapeDtypeStruct((1, XB), F32),
            jax.ShapeDtypeStruct((1, YB), F32),
            jax.ShapeDtypeStruct((1, XB), F32),
        ),
        in_specs=[pl.BlockSpec(memory_space=pltpu.HBM)] * 5,
        out_specs=(pl.BlockSpec(memory_space=pltpu.VMEM),) * 3,
        scratch_shapes=[
            pltpu.VMEM((DIM, XB), F32),
            pltpu.VMEM((DIM, YB), F32),
            pltpu.VMEM((1, YB), F32),
            pltpu.VMEM((1, XB), F32),
            pltpu.VMEM((1, YB), F32),
            pltpu.VMEM((NQ, DIM, XB), F32),
            pltpu.VMEM((NP, DIM + 8, YB), F32),
            pltpu.VMEM((NJ, 4 * DIM), BF16),
            pltpu.VMEM((NQ // 2, 4 * DIM, 2 * XB), BF16),
            pltpu.VMEM((NQ // 2, NJ, 2 * XB), F32),
            pltpu.VMEM((NQ // 2, 2, 8, 2 * XB), F32),
            pltpu.VMEM((NJ, 128), F32),
            pltpu.VMEM((NJ, 128), F32),
            pltpu.VMEM((2, YB, 128), F32),
            pltpu.VMEM((NQ, 1, 2 * XB), F32),
            pltpu.VMEM((NQ, 1, 2 * XB), F32),
            pltpu.VMEM((NQ, 1, XB), F32),
            pltpu.VMEM((8, NI), F32),
            pltpu.VMEM((NP, 1, 2 * YB), F32),
            pltpu.VMEM((NP, 1, 2 * YB), F32),
            pltpu.VMEM((NP, 1, YB), F32),
            pltpu.VMEM((NQ, 1, XB), F32),
            pltpu.VMEM((NQ, 1, XB), F32),
            dma((5,)),
            dma((2 * NQ,)),
            dma((NQ, 2)),
            dma((NP,)),
            dma((NP,)),
            dma((NQ,)),
            dma((NQ,)),
            dma((NQ,)),
            dma((NQ,)),
            dma((NP,)),
            dma((NP,)),
            dma((NP,)),
            dma((NP,)),
            dma((NQ,)),
            dma((NQ,)),
        ],
        compiler_params=pltpu.CompilerParams(
            collective_id=0, has_side_effects=True, vmem_limit_bytes=46 * 1024 * 1024
        ),
    )(
        *[
            pltpu.with_memory_space_constraint(v, pltpu.HBM)
            for v in (
                measured,
                generated,
                previous.reshape(1, YB),
                row_weight.reshape(1, XB),
                col_weight.reshape(1, YB),
            )
        ]
    )
    row, col, gap = pl.pallas_call(
        put_results,
        out_shape=(
            jax.ShapeDtypeStruct((1, XB), F32),
            jax.ShapeDtypeStruct((1, YB), F32),
            jax.ShapeDtypeStruct((1, XB), F32),
        ),
        in_specs=[pl.BlockSpec(memory_space=pltpu.VMEM)] * 3,
        out_specs=(pl.BlockSpec(memory_space=pl.ANY),) * 3,
        scratch_shapes=[dma((3,))],
        compiler_params=pltpu.CompilerParams(vmem_limit_bytes=1024 * 1024),
    )(row, col, gap)
    return row.reshape(XB), col.reshape(YB), gap.reshape(XB)


def solution(mesh):
    placed = (
        P(None, ("row", "col")),
        P(None, ("col", "row")),
        P(("col", "row")),
        P(("row", "col")),
        P(("col", "row")),
    )
    return jax.shard_map(
        body,
        mesh=mesh,
        in_specs=placed,
        out_specs=(P(("row", "col")), P(("col", "row")), P(("row", "col"))),
        check_vma=False,
    )
```

time: 67.5 us -> 69.2 us (1.025)
  Pallas kernels: 66.5 us -> 68.5 us
    pallas_call x1, Pallas kernels: 65.9 us -> 67.9 us  [body(): pl.pallas_call(kernel, out_shape=(jax.ShapeDtypeStruct((1, XB), F32), jax...]
where the time goes in v5:
time: 69.2 us
  Pallas kernels  68.5 us (99%)
    pallas_call x1, Pallas kernels, body(): pl.pallas_call(kernel, out_shape=(jax.ShapeDtypeStruct((1, XB), F32), jax...  67.9 us

profile of v5, /device:TPU:1, one launch (start us, length us, event | category | flops | bytes accessed | tf_op | source)
XLA Modules:
  0.0 69.2 jit_solution(9425825397996741005)
XLA Ops:
  0.6 67.9 %shard_map.76 = (f32[1,256]{1,0:T(1,128)S(1)}, f32[1,128]{1,0:T(1,128)S(1)}, f32[1,256]{1,0:T(1,128)S(1)}) custom-call(f32[64,256]{1,0:T(8,128)} %measured_hbm.1, f32[64,128]{1,0:T(8,128)} %generated_hbm.1, f32[1,128]{1,0:T(1,128)} %bitcast.7, f32[1,256]{1,0:T(1,128)} %bitcast.6, f32[1,128]{1,0:T(1,128)} %bitcast.8), custom_call_target="tpu_custom_call" | custom-call | tf_op jit(solution)/shard_map/pallas_call | solution.py:465
  68.6 0.6 shard_map.77

commit v6 on v5

v6 whole, which is shorter than its diff:
```python
import functools
import math

import jax
import jax.numpy as jnp
from jax import lax
from jax.experimental import pallas as pl
from jax.experimental.pallas import tpu as pltpu
from jax.sharding import PartitionSpec as P

EPSILON = 0.1
LOG2E = 1.0 / math.log(2.0)
LN2 = math.log(2.0)
MESH = pl.DeviceIdType.MESH
F32 = jnp.float32
BF16 = jnp.bfloat16

GRID = {"z": 8, "y": 4, "xh": 2, "xl": 2}
XB = 256
YB = 128
DIM = 64


def kernel(
    measured_hbm,
    generated_hbm,
    previous_hbm,
    row_weight_hbm,
    col_weight_hbm,
    row_out,
    col_out,
    gap_out,
    measured,
    generated,
    previous,
    row_weight,
    col_weight,
    xraw,
    yraw,
    yt,
    xaug,
    scores,
    row8,
    cstat,
    sstat,
    gbuf,
    rl,
    rx,
    ry,
    rfull,
    cl,
    cc,
    cz,
    w,
    wx,
    wy,
    in_sem,
    x_send,
    x_recv,
    y_send,
    y_recv,
    rx_send,
    rx_recv,
    ry_send,
    ry_recv,
    cc_send,
    cc_recv,
    cz_send,
    cz_recv,
    wx_send,
    wx_recv,
    wy_send,
    wy_recv,
):
    NZ, NY, NXH, NXL = GRID["z"], GRID["y"], GRID["xh"], GRID["xl"]
    NX = NXH * NXL
    NQ, NP = NX * NY, NZ * 2
    NI = NQ * XB
    NL = NI // 128
    ndev = NQ * NP

    loads = [
        pltpu.make_async_copy(src, dst, in_sem.at[n])
        for n, (src, dst) in enumerate(
            [
                (generated_hbm, generated),
                (previous_hbm, previous),
                (col_weight_hbm, col_weight),
                (measured_hbm, measured),
                (row_weight_hbm, row_weight),
            ]
        )
    ]
    for c in loads:
        c.start()

    row = lax.axis_index("row")
    col = lax.axis_index("col")
    z = row // (NY * NXH)
    y = (row // NXH) % NY
    x = (row % NXH) * NXL + col // 2
    core = col % 2

    def device(dz, dy, dx, dc):
        zz, yy, xx = (z + dz) % NZ, (y + dy) % NY, (x + dx) % NX
        return ((zz * NY + yy) * NXH + xx // NXL, (xx % NXL) * 2 + (core + dc) % 2)

    def copy(src, dst, send, recv, dev):
        return pltpu.make_async_remote_copy(
            src_ref=src, dst_ref=dst, send_sem=send, recv_sem=recv, device_id=dev, device_id_type=MESH
        )

    def loop(lo, hi, fn):
        def step(k, carry):
            fn(k)
            return carry

        lax.fori_loop(lo, hi, step, 0)

    def others(size):
        return sorted(range(1, size), key=lambda d: min(d, size - d))

    def along_x(e):
        return device(0, 0, e, 0)

    def along_y(e):
        return device(0, e, 0, 0)

    def along_z(e):
        return device(e, 0, 0, 0)

    sibling = device(0, 0, 0, 1)
    partners = [along_x(e) for e in others(NX)] + [along_y(e) for e in others(NY)]
    partners += [along_z(e) for e in others(NZ)] + [sibling]
    barrier = pltpu.get_barrier_semaphore()
    for dev in partners:
        pl.semaphore_signal(barrier, inc=1, device_id=dev, device_id_type=MESH)

    for c in loads:
        c.wait()
    scale = 2.0 * LOG2E / EPSILON
    xraw[0, 0] = measured[...] * scale
    gen = generated[...]
    log_b = jnp.log(col_weight[...]) - math.log(YB * ndev)
    ysq = jnp.sum(gen * gen, axis=0, keepdims=True)
    u = (log_b + (previous[...] - ysq) / EPSILON) * LOG2E
    yraw[0, 0, 0:DIM] = gen
    yraw[0, 0, DIM : DIM + 8] = jnp.broadcast_to(u, (8, YB))
    log_a = jnp.log(row_weight[...]) - math.log(XB * ndev)
    xsq = jnp.sum(measured[...] * measured[...], axis=0, keepdims=True)
    xaug[:, 3 * DIM :] = jnp.ones((NQ // 2, DIM, 2 * XB), BF16)

    pl.semaphore_wait(barrier, len(partners))

    pending = []

    def send(src, dst, send_sem, recv_sem, dev):
        c = copy(src, dst, send_sem, recv_sem, dev)
        c.start()
        pending.append(c)

    def arrived(ref, send_sem, recv_sem):
        copy(ref, ref, send_sem, recv_sem, sibling).wait_recv()

    first, second = slice(0, DIM // 2), slice(DIM // 2, DIM)

    for e in others(NZ):
        back = (NZ - e) % NZ
        send(yraw.at[0, 0], yraw.at[back, 0], y_send.at[0, e], y_recv.at[back, 0], along_z(e))
    send(yraw.at[0, 0], yraw.at[0, 1], y_send.at[0, 0], y_recv.at[0, 1], sibling)
    for e in others(NX):
        back = (NX - e) % NX
        send(xraw.at[0, 0, first], xraw.at[0, back, first], x_send.at[0, e], x_recv.at[0, back], along_x(e))
        send(xraw.at[0, 0, second], xraw.at[back, 0, second], x_send.at[1, e], x_recv.at[1, back], along_y(e))
    for e in others(NX):
        back = (NX - e) % NX
        send(xraw.at[0, 0, second], xraw.at[0, back, second], x_send.at[2, e], x_recv.at[2, back], along_x(e))
        send(xraw.at[0, 0, first], xraw.at[back, 0, first], x_send.at[3, e], x_recv.at[3, back], along_y(e))

    def forward_x():
        for e in others(NX):
            arrived(xraw.at[0, e, first], x_send.at[0, e], x_recv.at[0, e])
            arrived(xraw.at[e, 0, second], x_send.at[1, e], x_recv.at[1, e])
        for e in others(NX):
            back = (NX - e) % NX
            send(xraw.at[0, 1:, first], xraw.at[back, 1:, first], x_send.at[4, e], x_recv.at[4, back], along_y(e))
            send(xraw.at[1:, 0, second], xraw.at[1:, back, second], x_send.at[5, e], x_recv.at[5, back], along_x(e))

    def split(v):
        hi = v.astype(BF16).astype(F32)
        return hi, v - hi

    sub128 = lax.broadcasted_iota(jnp.int32, (8, YB), 0)

    def turn_y(slot):
        hi, lo = split(yraw[slot // 2, slot % 2, 0:DIM])
        t1, rest = split(yraw[slot // 2, slot % 2, DIM : DIM + 8])
        t2, t3 = split(rest)
        extra = jnp.where(sub128 == 0, t1, jnp.where(sub128 == 1, t2, jnp.where(sub128 == 2, t3, 0.0)))
        at = slice(slot * YB, (slot + 1) * YB)
        yt[at, 0 : 2 * DIM] = jnp.concatenate([hi, hi], axis=0).T.astype(BF16)
        yt[at, 2 * DIM :] = jnp.concatenate([lo, extra, jnp.zeros((DIM - 8, YB), F32)], axis=0).T.astype(BF16)

    def ready_x(pair):
        for h in range(2):
            v = xraw[pair // (NX // 2), (pair % (NX // 2)) * 2 + h]
            hi = v.astype(BF16)
            lo = (v - hi.astype(F32)).astype(BF16)
            at = slice(h * XB, (h + 1) * XB)
            xaug[pair, 0:DIM, at] = hi
            xaug[pair, DIM : 2 * DIM, at] = lo
            xaug[pair, 2 * DIM : 3 * DIM, at] = hi

    CH = 2 * YB
    PW = 2 * XB
    NPAIR = NQ // 2

    def rows_at(c):
        return pl.ds(pl.multiple_of(c * CH, CH), CH)

    def dot_stage(pair, c):
        scores[pair, rows_at(c)] = jnp.dot(yt[rows_at(c)], xaug[pair], preferred_element_type=F32)

    def max_stage(pair, c, accs):
        block = scores.at[pair, rows_at(c)]
        accs = list(accs)
        for k in range(CH // 8):
            accs[k % 2] = jnp.maximum(accs[k % 2], block[k * 8 : k * 8 + 8])
        return accs

    def exp_stage(pair, c, top, accs):
        block = scores.at[pair, rows_at(c)]
        accs = list(accs)
        for k in range(CH // 8):
            accs[k % 2] = accs[k % 2] + jnp.exp2(block[k * 8 : k * 8 + 8] - top)
        return accs

    turn_y(0)
    batches = [(1, 3), (NZ - 2, NZ), (3, NZ - 2)] if NZ == 8 else [(1, NZ)]
    for n in range(len(batches) + 1):
        if n < len(batches):
            lo, hi = batches[n]
            for dz in range(lo, hi):
                arrived(yraw.at[dz, 0], y_send.at[0, dz], y_recv.at[dz, 0])
            send(yraw.at[lo:hi, 0], yraw.at[lo:hi, 1], y_send.at[1, lo], y_recv.at[lo, 1], sibling)
            for dz in range(lo, hi):
                turn_y(2 * dz)
        if n == 0:
            forward_x()
            for e in others(NX):
                arrived(xraw.at[0, e, second], x_send.at[2, e], x_recv.at[2, e])
            ready_x(0)
            if NX > 2:
                ready_x(1)
            arrived(yraw.at[0, 1], y_send.at[0, 0], y_recv.at[0, 1])
            turn_y(1)
            dot_stage(0, 0)
        else:
            lo, hi = batches[n - 1]
            arrived(yraw.at[lo:hi, 1], y_send.at[1, lo], y_recv.at[lo, 1])
            for dz in range(lo, hi):
                turn_y(2 * dz + 1)
            for dz in range(lo, hi):
                dot_stage(0, dz)

    low = jnp.full((8, PW), -3e38, F32)
    zero = jnp.zeros((8, PW), F32)

    def row_step(one, two, three, top):
        def chunk(c, carry):
            tops, sums = carry[:2], carry[2:]
            if three is not None:
                sums = exp_stage(three, c, top, sums)
            if two is not None:
                tops = max_stage(two, c, tops)
            if one is not None:
                dot_stage(one, c)
            return (*tops, *sums)

        out = lax.fori_loop(0, NZ, chunk, (low, low, zero, zero), unroll=NZ)
        if three is not None:
            row8[three, 0] = top
            row8[three, 1] = out[2] + out[3]
        return jnp.maximum(out[0], out[1])

    def row_loop(step, top):
        ready_x(step)
        return row_step(step, step - 1, step - 2, top)

    def last_x():
        for e in others(NX):
            arrived(xraw.at[e, 0, first], x_send.at[3, e], x_recv.at[3, e])
            arrived(xraw.at[e, 1:, first], x_send.at[4, e], x_recv.at[4, e])
            arrived(xraw.at[1:, e, second], x_send.at[5, e], x_recv.at[5, e])

    if NX == 2:
        last_x()
        ready_x(1)
    top = row_step(1, 0, None, None)
    if NX > 2:
        last_x()
    top = lax.fori_loop(2, NPAIR, row_loop, top)
    top = row_step(None, NPAIR - 1, NPAIR - 2, top)
    row_step(None, None, NPAIR - 1, top)

    def log2(v):
        return jnp.log(v) * LOG2E

    def lse(values):
        best = functools.reduce(jnp.maximum, values)
        return best + log2(functools.reduce(jnp.add, [jnp.exp2(v - best) for v in values]))

    for pair in range(NPAIR):
        best = jnp.max(row8[pair, 0], axis=0, keepdims=True)
        local = best + log2(jnp.sum(row8[pair, 1] * jnp.exp2(row8[pair, 0] - best), axis=0, keepdims=True))
        for h in range(2):
            rl[0, 2 * pair + h] = local[:, h * XB : (h + 1) * XB]
    rl[0, NQ] = log_a * LOG2E
    for e in others(NX):
        back = (NX - e) % NX
        send(rl.at[0, 0 : NQ + 1], rx.at[back], rx_send.at[e], rx_recv.at[back], along_x(e))
    for e in others(NX):
        arrived(rx.at[e], rx_send.at[e], rx_recv.at[e])
    for dy in range(NY):
        for dx in range(NX):
            rl[1, dy * NX + dx] = lse(
                [rl[0, dy * NX + dx]] + [rx[e, dy * NX + (dx - e) % NX] for e in range(1, NX)]
            )
    rl[1, NQ] = rl[0, NQ]
    for e in range(1, NX):
        rl[1, NQ + e] = rx[e, NQ]
    for e in others(NY):
        back = (NY - e) % NY
        send(rl.at[1], ry.at[back], ry_send.at[e], ry_recv.at[back], along_y(e))
    for e in others(NY):
        arrived(ry.at[e], ry_send.at[e], ry_recv.at[e])
    for dy in range(NY):
        for dx in range(NX):
            k = dy * NX + dx
            full = lse([rl[1, k]] + [ry[e, ((dy - e) % NY) * NX + dx] for e in range(1, NY)])
            mass = rl[1, NQ + dx] if dy == 0 else ry[dy, NQ + dx]
            rfull[:, k * XB : (k + 1) * XB] = jnp.broadcast_to(mass - full, (8, XB))
            if k == 0:
                row_out[...] = xsq - (EPSILON * LN2) * full

    eye = lax.broadcasted_iota(jnp.int32, (YB, YB), 0) == lax.broadcasted_iota(jnp.int32, (YB, YB), 1)
    per = PW // 128

    def across(v):
        return jnp.sum(jnp.where(eye, v, 0.0), axis=0, keepdims=True)

    def rows_of(b):
        return pl.ds(pl.multiple_of(b * YB, YB), YB)

    def lanes(l):
        return slice((l % per) * 128, (l % per + 1) * 128)

    def col_tiles(b):
        blocks = [scores.at[pair, rows_of(b)] for pair in range(NPAIR)]
        cblock, sblock = cstat.at[rows_of(b)], sstat.at[rows_of(b)]
        for t in range(YB // 8):
            r8 = slice(t * 8, (t + 1) * 8)
            vals = [blocks[l // per][r8, lanes(l)] + rfull[:, l * 128 : (l + 1) * 128] for l in range(NL)]
            tops = vals
            while len(tops) > 1:
                tops = [jnp.maximum(tops[i], tops[i + 1]) for i in range(0, len(tops), 2)]
            top = tops[0]
            sums = [None] * 4
            for l in range(NL):
                e = jnp.exp2(vals[l] - top)
                blocks[l // per][r8, lanes(l)] = e
                sums[l % 4] = e if l < 4 else sums[l % 4] + e
            cblock[r8] = top
            sblock[r8] = (sums[0] + sums[1]) + (sums[2] + sums[3])

    def put_stats(b):
        c = cstat[rows_of(b), :]
        best = jnp.max(c, axis=1, keepdims=True)
        summed = jnp.sum(sstat[rows_of(b), :] * jnp.exp2(c - best), axis=1, keepdims=True)
        cl[0, b] = across(best) + log2(across(summed))

    def col_loop(b):
        put_stats(b - 1)
        col_tiles(b)

    col_tiles(0)
    loop(1, NP, col_loop)
    put_stats(NP - 1)

    cl[0, NP] = log_b * LOG2E
    send(cl.at[0, 0 : NP + 1], cc, cc_send, cc_recv, sibling)
    arrived(cc, cc_send, cc_recv)
    for dz in range(NZ):
        for dc in range(2):
            cl[1, 2 * dz + dc] = lse([cl[0, 2 * dz + dc], cc[2 * dz + 1 - dc]])
    cl[1, NP] = cl[0, NP]
    cl[1, NP + 1] = cc[NP]
    for e in others(NZ):
        back = (NZ - e) % NZ
        send(cl.at[1], cz.at[back], cz_send.at[e], cz_recv.at[back], along_z(e))
    for e in others(NZ):
        arrived(cz.at[e], cz_send.at[e], cz_recv.at[e])
    for dz in range(NZ):
        for dc in range(2):
            k = 2 * dz + dc
            full = lse([cl[1, k]] + [cz[e, 2 * ((dz - e) % NZ) + dc] for e in range(1, NZ)])
            mass = cl[1, NP + dc] if dz == 0 else cz[dz, NP + dc]
            cl[2, k] = mass - full
            if k == 0:
                col_out[...] = previous[...] + EPSILON * log_b - (EPSILON * LN2) * full

    def factors(b):
        q = jnp.sum(jnp.where(eye, cl[2, b], 0.0), axis=1, keepdims=True)
        gbuf[b % 2] = jnp.exp2(cstat[rows_of(b), :] + q)

    def gap_loop(b, acc):
        blocks = [scores.at[pair, rows_of(b)] for pair in range(NPAIR)]
        gblock = gbuf.at[b % 2]
        for t in range(YB // 8):
            r8 = slice(t * 8, (t + 1) * 8)
            g = gblock[r8]
            acc = [acc[l] + blocks[l // per][r8, lanes(l)] * g for l in range(NL)]
            if t == YB // 16:
                factors(jnp.minimum(b + 1, NP - 1))
        return acc

    factors(0)
    acc = lax.fori_loop(0, NP, gap_loop, [jnp.zeros((8, 128), F32) for _ in range(NL)])
    for k in range(NQ):
        for h in range(2):
            w[k // NX, k % NX, :, h * 128 : (h + 1) * 128] = jnp.sum(acc[2 * k + h], axis=0, keepdims=True)
    for e in others(NX):
        back = (NX - e) % NX
        send(w.at[:, e], wx.at[back], wx_send.at[e], wx_recv.at[back], along_x(e))
    for e in others(NX):
        arrived(wx.at[e], wx_send.at[e], wx_recv.at[e])
    for dy in range(NY):
        w[dy, 0] = functools.reduce(jnp.add, [w[dy, 0]] + [wx[e, dy] for e in range(1, NX)])
    for e in others(NY):
        back = (NY - e) % NY
        send(w.at[e, 0], wy.at[back], wy_send.at[e], wy_recv.at[back], along_y(e))
    for e in others(NY):
        arrived(wy.at[e], wy_send.at[e], wy_recv.at[e])
    gap_out[...] = jnp.log(functools.reduce(jnp.add, [w[0, 0]] + [wy[e] for e in range(1, NY)])) - log_a

    for c in pending:
        c.wait_send()


def put_results(row, col, gap, row_out, col_out, gap_out, sem):
    copies = [
        pltpu.make_async_copy(src, dst, sem.at[n])
        for n, (src, dst) in enumerate([(row, row_out), (col, col_out), (gap, gap_out)])
    ]
    for c in copies:
        c.start()
    for c in copies:
        c.wait()


def body(measured, generated, previous, row_weight, col_weight):
    NZ, NY, NX = GRID["z"], GRID["y"], GRID["xh"] * GRID["xl"]
    NQ, NP = NX * NY, NZ * 2
    NJ, NI = NP * YB, NQ * XB
    dma = pltpu.SemaphoreType.DMA
    row, col, gap = pl.pallas_call(
        kernel,
        out_shape=(
            jax.ShapeDtypeStruct((1, XB), F32),
            jax.ShapeDtypeStruct((1, YB), F32),
            jax.ShapeDtypeStruct((1, XB), F32),
        ),
        in_specs=[pl.BlockSpec(memory_space=pltpu.HBM)] * 5,
        out_specs=(pl.BlockSpec(memory_space=pltpu.VMEM),) * 3,
        scratch_shapes=[
            pltpu.VMEM((DIM, XB), F32),
            pltpu.VMEM((DIM, YB), F32),
            pltpu.VMEM((1, YB), F32),
            pltpu.VMEM((1, XB), F32),
            pltpu.VMEM((1, YB), F32),
            pltpu.VMEM((NY, NX, DIM, XB), F32),
            pltpu.VMEM((NZ, 2, DIM + 8, YB), F32),
            pltpu.VMEM((NJ, 4 * DIM), BF16),
            pltpu.VMEM((NQ // 2, 4 * DIM, 2 * XB), BF16),
            pltpu.VMEM((NQ // 2, NJ, 2 * XB), F32),
            pltpu.VMEM((NQ // 2, 2, 8, 2 * XB), F32),
            pltpu.VMEM((NJ, 128), F32),
            pltpu.VMEM((NJ, 128), F32),
            pltpu.VMEM((2, YB, 128), F32),
            pltpu.VMEM((2, NQ + NX, 1, XB), F32),
            pltpu.VMEM((NX, NQ + 1, 1, XB), F32),
            pltpu.VMEM((NY, NQ + NX, 1, XB), F32),
            pltpu.VMEM((8, NI), F32),
            pltpu.VMEM((3, NP + 2, 1, YB), F32),
            pltpu.VMEM((NP + 1, 1, YB), F32),
            pltpu.VMEM((NZ, NP + 2, 1, YB), F32),
            pltpu.VMEM((NY, NX, 1, XB), F32),
            pltpu.VMEM((NX, NY, 1, XB), F32),
            pltpu.VMEM((NY, 1, XB), F32),
            dma((5,)),
            dma((6, NX)),
            dma((6, NX)),
            dma((2, NZ)),
            dma((NZ, 2)),
            dma((NX,)),
            dma((NX,)),
            dma((NY,)),
            dma((NY,)),
            dma,
            dma,
            dma((NZ,)),
            dma((NZ,)),
            dma((NX,)),
            dma((NX,)),
            dma((NY,)),
            dma((NY,)),
        ],
        compiler_params=pltpu.CompilerParams(
            collective_id=0, has_side_effects=True, vmem_limit_bytes=46 * 1024 * 1024
        ),
    )(
        *[
            pltpu.with_memory_space_constraint(v, pltpu.HBM)
            for v in (
                measured,
                generated,
                previous.reshape(1, YB),
                row_weight.reshape(1, XB),
                col_weight.reshape(1, YB),
            )
        ]
    )
    row, col, gap = pl.pallas_call(
        put_results,
        out_shape=(
            jax.ShapeDtypeStruct((1, XB), F32),
            jax.ShapeDtypeStruct((1, YB), F32),
            jax.ShapeDtypeStruct((1, XB), F32),
        ),
        in_specs=[pl.BlockSpec(memory_space=pltpu.VMEM)] * 3,
        out_specs=(pl.BlockSpec(memory_space=pl.ANY),) * 3,
        scratch_shapes=[dma((3,))],
        compiler_params=pltpu.CompilerParams(vmem_limit_bytes=1024 * 1024),
    )(row, col, gap)
    return row.reshape(XB), col.reshape(YB), gap.reshape(XB)


def solution(mesh):
    placed = (
        P(None, ("row", "col")),
        P(None, ("col", "row")),
        P(("col", "row")),
        P(("row", "col")),
        P(("col", "row")),
    )
    return jax.shard_map(
        body,
        mesh=mesh,
        in_specs=placed,
        out_specs=(P(("row", "col")), P(("col", "row")), P(("row", "col"))),
        check_vma=False,
    )
```

time: 69.2 us -> 65.3 us (0.944)
  Pallas kernels: 68.5 us -> 64.5 us
    pallas_call x1, Pallas kernels: 67.9 us -> 63.9 us  [body(): pl.pallas_call(kernel, out_shape=(jax.ShapeDtypeStruct((1, XB), F32), jax...]
where the time goes in v6:
time: 65.3 us; the launch traced here: 65.1 us
  Pallas kernels  64.5 us (99%)
    pallas_call x1, Pallas kernels, body(): pl.pallas_call(kernel, out_shape=(jax.ShapeDtypeStruct((1, XB), F32), jax...  63.9 us

profile of v6, /device:TPU:1, one launch (start us, length us, event | category | flops | bytes accessed | tf_op | source)
XLA Modules:
  0.0 65.1 jit_solution(17332243903575345043)
XLA Ops:
  0.6 63.9 %shard_map.76 = (f32[1,256]{1,0:T(1,128)S(1)}, f32[1,128]{1,0:T(1,128)S(1)}, f32[1,256]{1,0:T(1,128)S(1)}) custom-call(f32[64,256]{1,0:T(8,128)} %measured_hbm.1, f32[64,128]{1,0:T(8,128)} %generated_hbm.1, f32[1,128]{1,0:T(1,128)} %bitcast.7, f32[1,256]{1,0:T(1,128)} %bitcast.6, f32[1,128]{1,0:T(1,128)} %bitcast.8), custom_call_target="tpu_custom_call" | custom-call | tf_op jit(solution)/shard_map/pallas_call | solution.py:466
  64.5 0.6 shard_map.77

commit v7 on v6

--- a/solution.py
+++ b/solution.py
@@ -162,29 +162,62 @@
     def arrived(ref, send_sem, recv_sem):
         copy(ref, ref, send_sem, recv_sem, sibling).wait_recv()
 
-    first, second = slice(0, DIM // 2), slice(DIM // 2, DIM)
-
-    for e in others(NZ):
-        back = (NZ - e) % NZ
-        send(yraw.at[0, 0], yraw.at[back, 0], y_send.at[0, e], y_recv.at[back, 0], along_z(e))
-    send(yraw.at[0, 0], yraw.at[0, 1], y_send.at[0, 0], y_recv.at[0, 1], sibling)
-    for e in others(NX):
-        back = (NX - e) % NX
-        send(xraw.at[0, 0, first], xraw.at[0, back, first], x_send.at[0, e], x_recv.at[0, back], along_x(e))
-        send(xraw.at[0, 0, second], xraw.at[back, 0, second], x_send.at[1, e], x_recv.at[1, back], along_y(e))
-    for e in others(NX):
-        back = (NX - e) % NX
-        send(xraw.at[0, 0, second], xraw.at[0, back, second], x_send.at[2, e], x_recv.at[2, back], along_x(e))
-        send(xraw.at[0, 0, first], xraw.at[back, 0, first], x_send.at[3, e], x_recv.at[3, back], along_y(e))
-
-    def forward_x():
-        for e in others(NX):
-            arrived(xraw.at[0, e, first], x_send.at[0, e], x_recv.at[0, e])
-            arrived(xraw.at[e, 0, second], x_send.at[1, e], x_recv.at[1, e])
-        for e in others(NX):
-            back = (NX - e) % NX
-            send(xraw.at[0, 1:, first], xraw.at[back, 1:, first], x_send.at[4, e], x_recv.at[4, back], along_y(e))
-            send(xraw.at[1:, 0, second], xraw.at[1:, back, second], x_send.at[5, e], x_recv.at[5, back], along_x(e))
+    def cuts(lo, hi, mid):
+        return {None: slice(lo, hi), 0: slice(lo, mid), 1: slice(mid, hi)}
+
+    ax, bx = cuts(0, DIM // 2, DIM // 4), cuts(DIM // 2, DIM, 3 * DIM // 4)
+    yrows = cuts(0, DIM + 8, 40)
+
+    def ring_send(d, n, ref, send_sem, recv_sem, along):
+        to = d + 1
+        if 2 * to < n:
+            send(ref(d, None), ref(to, None), send_sem.at[2 * d], recv_sem.at[to], along(n - 1))
+            send(ref((n - d) % n, None), ref(n - to, None), send_sem.at[2 * d + 1], recv_sem.at[n - to], along(1))
+        elif 2 * to == n:
+            send(ref(d, 0), ref(to, 0), send_sem.at[2 * d], recv_sem.at[to], along(n - 1))
+            send(ref((n - d) % n, 1), ref(to, 1), send_sem.at[2 * d + 1], recv_sem.at[0], along(1))
+
+    def ring_wait(d, n, ref, send_sem, recv_sem):
+        to = d + 1
+        if 2 * to < n:
+            arrived(ref(to, None), send_sem.at[0], recv_sem.at[to])
+            arrived(ref(n - to, None), send_sem.at[0], recv_sem.at[n - to])
+        elif 2 * to == n:
+            arrived(ref(to, 0), send_sem.at[0], recv_sem.at[to])
+            arrived(ref(to, 1), send_sem.at[0], recv_sem.at[0])
+
+    def y_ring(s, part):
+        return yraw.at[s, 0, yrows[part]]
+
+    x_rings = [
+        (NX, lambda s, part: xraw.at[0, s, ax[part]], along_x),
+        (NY, lambda s, part: xraw.at[s, 0, bx[part]], along_y),
+        (NX, lambda s, part: xraw.at[0, s, bx[part]], along_x),
+        (NY, lambda s, part: xraw.at[s, 0, ax[part]], along_y),
+        (NY, lambda s, part: xraw.at[s, 1:, ax[part]], along_y),
+        (NX, lambda s, part: xraw.at[1:, s, bx[part]], along_x),
+        (NY, lambda s, part: xraw.at[s, :, ax[part]], along_y),
+        (NX, lambda s, part: xraw.at[:, s, bx[part]], along_x),
+    ]
+
+    def x_go(r, d):
+        n, ref, along = x_rings[r]
+        ring_send(d, n, ref, x_send.at[r], x_recv.at[r], along)
+
+    def x_wait(r, d):
+        n, ref, along = x_rings[r]
+        ring_wait(d, n, ref, x_send.at[r], x_recv.at[r])
+
+    def y_go(d):
+        ring_send(d, NZ, y_ring, y_send.at[0], y_recv.at[0], along_z)
+
+    def y_wait(d):
+        ring_wait(d, NZ, y_ring, y_send.at[0], y_recv.at[0])
+
+    y_go(0)
+    send(yraw.at[0, 0], yraw.at[0, 1], y_send.at[1, 0], y_recv.at[1, 0], sibling)
+    for r in range(4):
+        x_go(r, 0)
 
     def split(v):
         hi = v.astype(BF16).astype(F32)
@@ -218,9 +251,6 @@
     def rows_at(c):
         return pl.ds(pl.multiple_of(c * CH, CH), CH)
 
-    def dot_stage(pair, c):
-        scores[pair, rows_at(c)] = jnp.dot(yt[rows_at(c)], xaug[pair], preferred_element_type=F32)
-
     def max_stage(pair, c, accs):
         block = scores.at[pair, rows_at(c)]
         accs = list(accs)
@@ -235,73 +265,75 @@
             accs[k % 2] = accs[k % 2] + jnp.exp2(block[k * 8 : k * 8 + 8] - top)
         return accs
 
+    def dots(pair, lo, hi):
+        at = slice(lo * CH, hi * CH)
+        scores[pair, at] = jnp.dot(yt[at], xaug[pair], preferred_element_type=F32)
+
+    def sibling_wait(dz):
+        arrived(yraw.at[dz, 1], y_send.at[1, 0], y_recv.at[1, dz])
+        turn_y(2 * dz + 1)
+
     turn_y(0)
-    batches = [(1, 3), (NZ - 2, NZ), (3, NZ - 2)] if NZ == 8 else [(1, NZ)]
-    for n in range(len(batches) + 1):
-        if n < len(batches):
-            lo, hi = batches[n]
-            for dz in range(lo, hi):
-                arrived(yraw.at[dz, 0], y_send.at[0, dz], y_recv.at[dz, 0])
-            send(yraw.at[lo:hi, 0], yraw.at[lo:hi, 1], y_send.at[1, lo], y_recv.at[lo, 1], sibling)
-            for dz in range(lo, hi):
-                turn_y(2 * dz)
-        if n == 0:
-            forward_x()
-            for e in others(NX):
-                arrived(xraw.at[0, e, second], x_send.at[2, e], x_recv.at[2, e])
+    for d in range(NZ // 2):
+        y_wait(d)
+        y_go(d + 1)
+        got = sorted({d + 1, NZ - d - 1})
+        for dz in got:
+            send(yraw.at[dz, 0], yraw.at[dz, 1], y_send.at[1, dz], y_recv.at[1, dz], sibling)
+        if d == 0:
+            for r in (0, 1):
+                x_wait(r, 0)
+                x_go(r, 1)
+        if d == min(1, NZ // 2 - 1):
+            for r in (0, 1):
+                x_wait(r, 1)
+                x_go(4 + r, 0)
+        for dz in got:
+            turn_y(2 * dz)
+        if d == 0:
+            sibling_wait(0)
+            x_wait(2, 0)
             ready_x(0)
-            if NX > 2:
-                ready_x(1)
-            arrived(yraw.at[0, 1], y_send.at[0, 0], y_recv.at[0, 1])
-            turn_y(1)
-            dot_stage(0, 0)
+            dots(0, 0, 1)
         else:
-            lo, hi = batches[n - 1]
-            arrived(yraw.at[lo:hi, 1], y_send.at[1, lo], y_recv.at[lo, 1])
-            for dz in range(lo, hi):
-                turn_y(2 * dz + 1)
-            for dz in range(lo, hi):
-                dot_stage(0, dz)
-
+            for dz in (d, NZ - d):
+                sibling_wait(dz)
+            dots(0, d, d + 1)
+            dots(0, NZ - d, NZ - d + 1)
+    for r in (3, 4, 5):
+        x_wait(r, 0)
+    for r in (6, 7):
+        x_go(r, 1)
+    sibling_wait(NZ // 2)
+    dots(0, NZ // 2, NZ // 2 + 1)
     low = jnp.full((8, PW), -3e38, F32)
     zero = jnp.zeros((8, PW), F32)
 
     def row_step(one, two, three, top):
-        def chunk(c, carry):
-            tops, sums = carry[:2], carry[2:]
+        tops, sums = (low, low), (zero, zero)
+        for c in range(NZ):
+            if one is not None and c % 4 == 0:
+                dots(one, c, min(c + 4, NZ))
             if three is not None:
                 sums = exp_stage(three, c, top, sums)
             if two is not None:
                 tops = max_stage(two, c, tops)
-            if one is not None:
-                dot_stage(one, c)
-            return (*tops, *sums)
-
-        out = lax.fori_loop(0, NZ, chunk, (low, low, zero, zero), unroll=NZ)
         if three is not None:
             row8[three, 0] = top
-            row8[three, 1] = out[2] + out[3]
-        return jnp.maximum(out[0], out[1])
-
-    def row_loop(step, top):
-        ready_x(step)
-        return row_step(step, step - 1, step - 2, top)
-
-    def last_x():
-        for e in others(NX):
-            arrived(xraw.at[e, 0, first], x_send.at[3, e], x_recv.at[3, e])
-            arrived(xraw.at[e, 1:, first], x_send.at[4, e], x_recv.at[4, e])
-            arrived(xraw.at[1:, e, second], x_send.at[5, e], x_recv.at[5, e])
-
-    if NX == 2:
-        last_x()
-        ready_x(1)
-    top = row_step(1, 0, None, None)
-    if NX > 2:
-        last_x()
-    top = lax.fori_loop(2, NPAIR, row_loop, top)
-    top = row_step(None, NPAIR - 1, NPAIR - 2, top)
-    row_step(None, None, NPAIR - 1, top)
+            row8[three, 1] = sums[0] + sums[1]
+        return jnp.maximum(*tops)
+
+    early = [0] + ([NX // 2, NPAIR - NX // 2] if NX > 2 else [])
+    pairs = early + [p for p in range(NPAIR) if p not in early]
+    top = None
+    for step in range(1, NPAIR + 2):
+        if step == len(early):
+            for r in (6, 7):
+                x_wait(r, 1)
+        one, two, three = [pairs[k] if 0 <= k < NPAIR else None for k in (step, step - 1, step - 2)]
+        if one is not None:
+            ready_x(one)
+        top = row_step(one, two, three, top)
 
     def log2(v):
         return jnp.log(v) * LOG2E
@@ -498,10 +530,10 @@
             pltpu.VMEM((NX, NY, 1, XB), F32),
             pltpu.VMEM((NY, 1, XB), F32),
             dma((5,)),
-            dma((6, NX)),
-            dma((6, NX)),
+            dma((8, NX)),
+            dma((8, NX)),
             dma((2, NZ)),
-            dma((NZ, 2)),
+            dma((2, NZ)),
             dma((NX,)),
             dma((NX,)),
             dma((NY,)),

time: 65.3 us -> 67.4 us (1.032)
  Pallas kernels: 64.5 us -> 66.7 us
    pallas_call x1, Pallas kernels: 63.9 us -> 66.1 us  [body(): pl.pallas_call(kernel, out_shape=(jax.ShapeDtypeStruct((1, XB), F32), jax...]
where the time goes in v7:
time: 67.4 us; the launch traced here: 67.3 us
  Pallas kernels  66.7 us (99%)
    pallas_call x1, Pallas kernels, body(): pl.pallas_call(kernel, out_shape=(jax.ShapeDtypeStruct((1, XB), F32), jax...  66.1 us

profile of v7, /device:TPU:1, one launch (start us, length us, event | category | flops | bytes accessed | tf_op | source)
XLA Modules:
  0.0 67.3 jit_solution(9470495117644922142)
XLA Ops:
  0.6 66.1 %shard_map.76 = (f32[1,256]{1,0:T(1,128)S(1)}, f32[1,128]{1,0:T(1,128)S(1)}, f32[1,256]{1,0:T(1,128)S(1)}) custom-call(f32[64,256]{1,0:T(8,128)} %measured_hbm.1, f32[64,128]{1,0:T(8,128)} %generated_hbm.1, f32[1,128]{1,0:T(1,128)} %bitcast.7, f32[1,256]{1,0:T(1,128)} %bitcast.6, f32[1,128]{1,0:T(1,128)} %bitcast.8), custom_call_target="tpu_custom_call" | custom-call | tf_op jit(solution)/shard_map/pallas_call | solution.py:498
  66.7 0.6 shard_map.77

commit v8 on v6

--- a/solution.py
+++ b/solution.py
@@ -218,15 +218,16 @@
     def rows_at(c):
         return pl.ds(pl.multiple_of(c * CH, CH), CH)
 
-    def dot_stage(pair, c):
-        scores[pair, rows_at(c)] = jnp.dot(yt[rows_at(c)], xaug[pair], preferred_element_type=F32)
-
-    def max_stage(pair, c, accs):
-        block = scores.at[pair, rows_at(c)]
-        accs = list(accs)
+    low = jnp.full((8, PW), -3e38, F32)
+    zero = jnp.zeros((8, PW), F32)
+
+    def dot_stage(pair, c, tops):
+        res = jnp.dot(yt[rows_at(c)], xaug[pair], preferred_element_type=F32)
+        scores[pair, rows_at(c)] = res
+        tops = list(tops)
         for k in range(CH // 8):
-            accs[k % 2] = jnp.maximum(accs[k % 2], block[k * 8 : k * 8 + 8])
-        return accs
+            tops[k % 2] = jnp.maximum(tops[k % 2], res[k * 8 : k * 8 + 8])
+        return tops
 
     def exp_stage(pair, c, top, accs):
         block = scores.at[pair, rows_at(c)]
@@ -236,6 +237,7 @@
         return accs
 
     turn_y(0)
+    tops0 = [low, low]
     batches = [(1, 3), (NZ - 2, NZ), (3, NZ - 2)] if NZ == 8 else [(1, NZ)]
     for n in range(len(batches) + 1):
         if n < len(batches):
@@ -254,38 +256,28 @@
                 ready_x(1)
             arrived(yraw.at[0, 1], y_send.at[0, 0], y_recv.at[0, 1])
             turn_y(1)
-            dot_stage(0, 0)
+            tops0 = dot_stage(0, 0, tops0)
         else:
             lo, hi = batches[n - 1]
             arrived(yraw.at[lo:hi, 1], y_send.at[1, lo], y_recv.at[lo, 1])
             for dz in range(lo, hi):
                 turn_y(2 * dz + 1)
             for dz in range(lo, hi):
-                dot_stage(0, dz)
-
-    low = jnp.full((8, PW), -3e38, F32)
-    zero = jnp.zeros((8, PW), F32)
-
-    def row_step(one, two, three, top):
-        def chunk(c, carry):
-            tops, sums = carry[:2], carry[2:]
-            if three is not None:
-                sums = exp_stage(three, c, top, sums)
-            if two is not None:
-                tops = max_stage(two, c, tops)
+                tops0 = dot_stage(0, dz, tops0)
+
+    def row_step(one, two, top):
+        tops, sums = (low, low), (zero, zero)
+        for c in range(NZ):
+            sums = exp_stage(two, c, top, sums)
             if one is not None:
-                dot_stage(one, c)
-            return (*tops, *sums)
-
-        out = lax.fori_loop(0, NZ, chunk, (low, low, zero, zero), unroll=NZ)
-        if three is not None:
-            row8[three, 0] = top
-            row8[three, 1] = out[2] + out[3]
-        return jnp.maximum(out[0], out[1])
+                tops = dot_stage(one, c, tops)
+        row8[two, 0] = top
+        row8[two, 1] = sums[0] + sums[1]
+        return jnp.maximum(*tops)
 
     def row_loop(step, top):
         ready_x(step)
-        return row_step(step, step - 1, step - 2, top)
+        return row_step(step, step - 1, top)
 
     def last_x():
         for e in others(NX):
@@ -296,12 +288,11 @@
     if NX == 2:
         last_x()
         ready_x(1)
-    top = row_step(1, 0, None, None)
+    top = row_step(1, 0, jnp.maximum(*tops0))
     if NX > 2:
         last_x()
     top = lax.fori_loop(2, NPAIR, row_loop, top)
-    top = row_step(None, NPAIR - 1, NPAIR - 2, top)
-    row_step(None, None, NPAIR - 1, top)
+    row_step(None, NPAIR - 1, top)
 
     def log2(v):
         return jnp.log(v) * LOG2E

time: 65.3 us -> 62.6 us (0.959)
  Pallas kernels: 64.5 us -> 61.8 us
    pallas_call x1, Pallas kernels: 63.9 us -> 61.2 us  [body(): pl.pallas_call(kernel, out_shape=(jax.ShapeDtypeStruct((1, XB), F32), jax...]
where the time goes in v8:
time: 62.6 us; the launch traced here: 62.5 us
  Pallas kernels  61.8 us (99%)
  between operations  0.64 us (1%)
    pallas_call x1, Pallas kernels, body(): pl.pallas_call(kernel, out_shape=(jax.ShapeDtypeStruct((1, XB), F32), jax...  61.2 us

profile of v8, /device:TPU:1, one launch (start us, length us, event | category | flops | bytes accessed | tf_op | source)
XLA Modules:
  0.0 62.5 jit_solution(4820293501591904915)
XLA Ops:
  0.6 61.2 %shard_map.76 = (f32[1,256]{1,0:T(1,128)S(1)}, f32[1,128]{1,0:T(1,128)S(1)}, f32[1,256]{1,0:T(1,128)S(1)}) custom-call(f32[64,256]{1,0:T(8,128)} %measured_hbm.1, f32[64,128]{1,0:T(8,128)} %generated_hbm.1, f32[1,128]{1,0:T(1,128)} %bitcast.7, f32[1,256]{1,0:T(1,128)} %bitcast.6, f32[1,128]{1,0:T(1,128)} %bitcast.8), custom_call_target="tpu_custom_call" | custom-call | tf_op jit(solution)/shard_map/pallas_call | solution.py:457
  61.9 0.6 shard_map.77

commit v9 on v8

--- a/solution.py
+++ b/solution.py
@@ -198,8 +198,8 @@
         t2, t3 = split(rest)
         extra = jnp.where(sub128 == 0, t1, jnp.where(sub128 == 1, t2, jnp.where(sub128 == 2, t3, 0.0)))
         at = slice(slot * YB, (slot + 1) * YB)
-        yt[at, 0 : 2 * DIM] = jnp.concatenate([hi, hi], axis=0).T.astype(BF16)
-        yt[at, 2 * DIM :] = jnp.concatenate([lo, extra, jnp.zeros((DIM - 8, YB), F32)], axis=0).T.astype(BF16)
+        yt[at, 0 : 2 * DIM] = jnp.concatenate([hi, hi], axis=0).astype(BF16).T
+        yt[at, 2 * DIM :] = jnp.concatenate([lo, extra, jnp.zeros((DIM - 8, YB), F32)], axis=0).astype(BF16).T
 
     def ready_x(pair):
         for h in range(2):
@@ -291,7 +291,8 @@
     top = row_step(1, 0, jnp.maximum(*tops0))
     if NX > 2:
         last_x()
-    top = lax.fori_loop(2, NPAIR, row_loop, top)
+    for step in range(2, NPAIR):
+        top = row_loop(step, top)
     row_step(None, NPAIR - 1, top)
 
     def log2(v):

time: 62.6 us -> 61.3 us (0.979)
  Pallas kernels: 61.8 us -> 60.5 us
    pallas_call x1, Pallas kernels: 61.2 us -> 59.9 us  [body(): pl.pallas_call(kernel, out_shape=(jax.ShapeDtypeStruct((1, XB), F32), jax...]
where the time goes in v9:
time: 61.3 us; the launch traced here: 61.2 us
  Pallas kernels  60.5 us (99%)
  between operations  0.64 us (1%)
    pallas_call x1, Pallas kernels, body(): pl.pallas_call(kernel, out_shape=(jax.ShapeDtypeStruct((1, XB), F32), jax...  59.9 us

profile of v9, /device:TPU:1, one launch (start us, length us, event | category | flops | bytes accessed | tf_op | source)
XLA Modules:
  0.0 61.2 jit_solution(11183796672306084852)
XLA Ops:
  0.6 59.9 %shard_map.76 = (f32[1,256]{1,0:T(1,128)S(1)}, f32[1,128]{1,0:T(1,128)S(1)}, f32[1,256]{1,0:T(1,128)S(1)}) custom-call(f32[64,256]{1,0:T(8,128)} %measured_hbm.1, f32[64,128]{1,0:T(8,128)} %generated_hbm.1, f32[1,128]{1,0:T(1,128)} %bitcast.7, f32[1,256]{1,0:T(1,128)} %bitcast.6, f32[1,128]{1,0:T(1,128)} %bitcast.8), custom_call_target="tpu_custom_call" | custom-call | tf_op jit(solution)/shard_map/pallas_call | solution.py:458
  60.6 0.6 shard_map.77
